TPU v7x, 32 devices: a whole 2x2x4 slice. The times are simulated.
32 devices in a mesh: lat: 16 (over z, x, core), lon: 2 (over y).
Axes of the slice: x: 2, y: 2, z: 4, core: 2. Of those that a mesh axis runs over, the one named last changes fastest.
Arguments:
- grid_input: bfloat16 [352, 1440, 256], P('lat', 'lon'), may hold values from -1.5 to 1.5
- cotangent: bfloat16 [352, 1440, 256], P('lat', 'lon'), may hold values from -6 to 6
- mixing: bfloat16 [192, 256, 256], P('lat', 'lon'), may hold values from -0.375 to 0.375
Outputs:
- input_grad: bfloat16 [352, 1440, 256], P('lat', 'lon')
- weight_grad: float32 [192, 256, 256], P('lat', 'lon')
All inputs are finite; a program needn't handle non-finite values.
Results may differ from a plain program's by a relative error of at most 0.0083.
Values may be sent and summed in bfloat16 or wider, within the bound.
A program may use at most 128 MiB of HBM per device.

v0:
```python
import math

import jax
import jax.numpy as jnp
from jax import lax
from jax.sharding import PartitionSpec as P


def quadrature(count_lat):
    colatitude = (jnp.arange(count_lat, dtype=jnp.float32) + 0.5) * (math.pi / count_lat)
    return math.pi / count_lat * jnp.sin(colatitude)


def degree_block():
    for width in (16, 8, 4, 2):
        return width
    return 1


def legendre_table(order_ids, count_lat, degrees, order_cap):
    colatitude = (jnp.arange(count_lat, dtype=jnp.float32) + 0.5) * (math.pi / count_lat)
    cosine = jnp.cos(colatitude)[None, :]
    sine_row = jnp.sin(colatitude)[None, :]
    order_value = order_ids.astype(jnp.float32)[:, None]
    counter = jnp.arange(1, order_cap + 1, dtype=jnp.float32)[None, :]
    log_terms = jnp.where(counter <= order_value, jnp.log1p(0.5 / counter), 0.0)
    log_start = (
        0.5 * math.log(0.5)
        + 0.5 * jnp.sum(log_terms, axis=1, keepdims=True)
        + order_value * jnp.log(sine_row)
    )
    zero_state = jnp.zeros((order_ids.shape[0], count_lat), jnp.float32)
    width = degree_block()

    def advance(carried, degree):
        previous, earlier, scale_log = carried
        growth = jnp.sqrt(
            (4.0 * degree * degree - 1.0)
            / jnp.maximum(degree * degree - order_value * order_value, 1.0)
        )
        shrink = jnp.sqrt(
            jnp.maximum((degree - 1.0) * (degree - 1.0) - order_value * order_value, 0.0)
            / jnp.maximum(4.0 * (degree - 1.0) * (degree - 1.0) - 1.0, 1.0)
        )
        recurred = growth * (cosine * previous - shrink * earlier)
        first_step = cosine * jnp.sqrt(2.0 * order_value + 3.0) * previous
        current = jnp.where(
            degree == order_value,
            1.0,
            jnp.where(
                degree == order_value + 1.0,
                first_step,
                jnp.where(degree > order_value, recurred, 0.0),
            ),
        )
        oversized = jnp.abs(current) > 10000000000.0
        factor = jnp.where(oversized, 1e-10, 1.0)
        scale_log = scale_log + jnp.where(oversized, math.log(10000000000.0), 0.0)
        current = current * factor
        stored = (current * jnp.exp(scale_log)).astype(jnp.bfloat16)
        return ((current, previous * factor, scale_log), stored)

    def advance_block(carried, block_start):
        stored_list = []
        for step in range(width):
            carried, stored = advance(carried, block_start + float(step))
            stored_list.append(stored)
        return (carried, jnp.stack(stored_list, axis=0))

    initial = (zero_state, zero_state, log_start)
    starts = jnp.arange(degrees // width, dtype=jnp.float32) * float(width)
    _, blocks = lax.scan(advance_block, initial, starts)
    return blocks.reshape(degrees, order_ids.shape[0], count_lat)


def fourier_tables(order_ids, count_lon):
    points = jnp.arange(count_lon, dtype=jnp.int32)
    phase_index = points[:, None] * order_ids[None, :] % count_lon
    angles = phase_index.astype(jnp.float32) * (2.0 * math.pi / count_lon)
    forward = jnp.stack([jnp.cos(angles), -jnp.sin(angles)], axis=2).reshape(
        count_lon, 2 * order_ids.shape[0]
    )
    factor = jnp.where(order_ids == 0, 1.0, 2.0).astype(jnp.float32) / count_lon
    backward = forward * jnp.repeat(factor, 2)[None, :]
    return (forward.astype(jnp.bfloat16), backward.astype(jnp.bfloat16))


def analyse(legendre, spectra):
    result = jnp.einsum("lmj,jmc->mlc", legendre, spectra, preferred_element_type=jnp.float32)
    return result.astype(jnp.bfloat16)


def synthesise(legendre, coeffs):
    result = jnp.einsum("lmj,mlc->jmc", legendre, coeffs, preferred_element_type=jnp.float32)
    return result


def local(grid_input, cotangent, mixing):
    lat_count = lax.axis_size("lat")
    lon_count = lax.axis_size("lon")
    lat_rows = grid_input.shape[0]
    count_lat = lat_rows * lat_count
    count_lon = grid_input.shape[1] * lon_count
    per_dev = mixing.shape[0]
    order_total = per_dev * lat_count
    block_ch = grid_input.shape[2] // lon_count
    lat_pos = lax.axis_index("lat")
    slot_ids = jnp.arange(order_total, dtype=jnp.int32)
    forward, backward = fourier_tables(slot_ids, count_lon)
    weights = quadrature(count_lat)
    own_weights = lax.dynamic_slice_in_dim(weights, lat_pos * lat_rows, lat_rows)
    columns_x, columns_g = (
        lax.all_to_all(grid_input, "lon", split_axis=2, concat_axis=1, tiled=True),
        lax.all_to_all(cotangent, "lon", split_axis=2, concat_axis=1, tiled=True),
    )
    spec_x = (
        jnp.einsum("jkc,kq->jqc", columns_x, forward, preferred_element_type=jnp.float32)
        * own_weights[:, None, None]
    ).astype(jnp.bfloat16)
    spec_g = jnp.einsum(
        "jkc,kq->jqc", columns_g, backward, preferred_element_type=jnp.float32
    ).astype(jnp.bfloat16)
    rows_x, rows_g = (
        lax.all_to_all(spec_x, "lat", split_axis=1, concat_axis=0, tiled=True),
        lax.all_to_all(spec_g, "lat", split_axis=1, concat_axis=0, tiled=True),
    )
    rows_x = rows_x.reshape(count_lat, per_dev, 2 * block_ch)
    rows_g = rows_g.reshape(count_lat, per_dev, 2 * block_ch)
    own_orders = lax.dynamic_slice_in_dim(slot_ids, lat_pos * per_dev, per_dev)
    legendre = legendre_table(own_orders, count_lat, order_total, order_total)
    coefficients = analyse(legendre, rows_x).reshape(per_dev, order_total, 2, block_ch)
    adjoint = analyse(legendre, rows_g).reshape(per_dev, order_total, 2, block_ch)
    full_adjoint = lax.all_gather(adjoint, "lon", axis=3, tiled=True)
    full_weights = lax.all_gather(mixing, "lat", axis=0, tiled=True)
    mixed_coeffs = jnp.einsum(
        "mlrc,lic->mlri", full_adjoint, full_weights, preferred_element_type=jnp.float32
    ).astype(jnp.bfloat16)
    grad_term = jnp.einsum(
        "mlri,mlrc->lic", coefficients, full_adjoint, preferred_element_type=jnp.float32
    )
    weight_grad = lax.psum_scatter(grad_term, "lat", scatter_dimension=0, tiled=True)
    mixed_coeffs = mixed_coeffs.reshape(per_dev, order_total, 2 * block_ch)
    back_rows = (synthesise(legendre, mixed_coeffs) * weights[:, None, None]).astype(jnp.bfloat16)
    back_rows = back_rows.reshape(count_lat, 2 * per_dev, block_ch)
    back_local = lax.all_to_all(back_rows, "lat", split_axis=0, concat_axis=1, tiled=True)
    grid_back = jnp.einsum(
        "jqc,kq->jkc", back_local, forward, preferred_element_type=jnp.float32
    ).astype(jnp.bfloat16)
    grid_local = lax.all_to_all(grid_back, "lon", split_axis=1, concat_axis=2, tiled=True)
    input_grad = (cotangent.astype(jnp.float32) + grid_local.astype(jnp.float32)).astype(
        jnp.bfloat16
    )
    return (input_grad, weight_grad)


def solution(mesh):
    in_specs = (P("lat", "lon", None), P("lat", "lon", None), P("lat", "lon", None))
    out_specs = (P("lat", "lon", None), P("lat", "lon", None))
    return jax.shard_map(local, mesh=mesh, in_specs=in_specs, out_specs=out_specs, check_vma=False)
```

profile of v0, /device:TPU:27, one launch (start us, length us, event | category | flops | bytes accessed | tf_op | source)
XLA Modules:
  0.0 953.5 jit_solution(15791024341065301500)
XLA Ops:
  7.2 12.8 %copy.82 = bf16[22,720,256]{1,0,2:T(8,128)(2,1)} copy(bf16[22,720,256]{2,1,0:T(8,128)(2,1)} %param.6) | data formatting | bytes 16220160 | tf_op args[1]
  20.0 7.3 all-to-all-start
  27.4 4.9 sine_negate_fusion
  35.9 94.4 %all-to-all-done = bf16[22,720,256]{1,0,2:T(8,128)(2,1)} async-done(((bf16[22,720,256]{1,0,2:T(8,128)(2,1)}), bf16[22,720,256]{1,0,2:T(8,128)(2,1)}, u32[]{:S(2)}, u32[]{:S(2)}) %all-to-all-start) | async-done | bytes 8110112 | tf_op jit(solution)/shard_map/all_to_all | solution.py:114
  130.3 12.5 %copy.83 = bf16[22,720,2,128]{3,1,2,0:T(8,128)(2,1)} copy(bf16[22,720,2,128]{1,0,3,2:T(8,128)(2,1)} %bitcast.5) | data formatting | bytes 16220160 | tf_op jit(solution)/shard_map/all_to_all | solution.py:114
  142.8 7.2 convert_bitcast_fusion.2
  150.0 2.8 copy.85
  152.8 7.3 all-to-all-start.1
  160.2 204.0 %while.23 = (s32[]{:T(128)}, f32[12,352]{1,0:T(8,128)S(1)}, f32[12,352]{1,0:T(8,128)S(1)}, f32[12,352]{1,0:T(8,128)S(1)}, bf16[12,16,12,352]{3,2,1,0:T(8,128)(2,...) while((s32[]{:T(128)}, f32[12,352]{1,0:T(8,128)S(1)}, ...), condition=%wide.region_2.3_spmd.clone.clone, body=%wide.region_1.2_spmd.clone.clone.sunk | while | flops 1818842 | bytes 2434092 | solution.py:72
  364.2 3.3 copy.133
  367.5 4.8 reshape.1185
  372.3 4.6 fusion.126
  376.9 2.8 reshape.1186
  383.0 12.9 %copy.98 = bf16[22,720,256]{1,0,2:T(8,128)(2,1)} copy(bf16[22,720,256]{2,1,0:T(8,128)(2,1)} %param.5) | data formatting | bytes 16220160 | tf_op args[0]
  395.9 7.4 all-to-all-start.4
  405.8 122.2 %all-to-all-done.4 = bf16[22,720,256]{1,0,2:T(8,128)(2,1)} async-done(((bf16[22,720,256]{1,0,2:T(8,128)(2,1)}), bf16[22,720,256]{1,0,2:T(8,128)(2,1)}, u32[]{:S(2)}, u32[]{:S(2)}) %all-to-all-start.4) | async-done | bytes 8110112 | tf_op jit(solution)/shard_map/all_to_all | solution.py:113
  528.0 12.1 %copy.99 = bf16[22,720,2,128]{3,1,2,0:T(8,128)(2,1)} copy(bf16[22,720,2,128]{1,0,3,2:T(8,128)(2,1)} %bitcast.23) | data formatting | bytes 16220160 | tf_op jit(solution)/shard_map/all_to_all | solution.py:113
  540.1 7.1 fusion.115
  548.6 58.5 %all_to_all.93 = bf16[22,384,128]{2,0,1:T(8,128)(2,1)S(1)} all-to-all(bf16[22,384,128]{2,0,1:T(8,128)(2,1)S(1)} %copy.101), channel_id=1, replica_groups=mesh['lat'=16,'lon'=2] {'lat'}, dimensions={1} | all-to-all | bytes 4325376 | tf_op jit(solution)/shard_map/all_to_all | solution.py:124
  609.7 3.6 fusion.129
  613.6 14.0 %convolution_bitcast_fusion = f32[192,128,256]{2,1,0:T(8,128)} fusion(bf16[12,192,2,256]{3,0,2,1:T(8,128)(2,1)} %all-gather.3.cloned.1.call-done, bf16[12,192,2,128]{3,2,1,0:T(2,128)(2,1)S(1)} %reshape.1190), kind=kOutput, calls=%fused_computation.313 | convolution fusion | flops 301989888 | bytes 28704768 | tf_op jit(solution)/shard_map/mlri,mlrc->lic/dot_general | solution.py:138
  629.5 9.0 fusion.132
  640.4 4.7 fusion.124
  645.1 3.2 copy.92
  651.1 96.7 %all_to_all.94 = bf16[352,24,128]{2,1,0:T(8,128)(2,1)S(1)} all-to-all(bf16[352,24,128]{2,1,0:T(8,128)(2,1)} %copy.93), channel_id=1, replica_groups=mesh['lat'=16,'lon'=2] {'lat'}, dimensions={0} | all-to-all | bytes 4325376 | tf_op jit(solution)/shard_map/all_to_all | solution.py:145
  749.1 4.9 convert_bitcast_fusion.1
  754.0 23.6 %copy.96 = bf16[22,1440,128]{2,0,1:T(8,128)(2,1)S(1)} copy(bf16[22,1440,128]{2,1,0:T(8,128)(2,1)S(1)} %convert_bitcast_fusion.1) | data formatting | bytes 16220160 | tf_op jit(solution)/shard_map/convert_element_type | solution.py:148
  777.6 102.0 %all_to_all.95 = bf16[22,1440,128]{2,0,1:T(8,128)(2,1)} all-to-all(bf16[22,1440,128]{2,0,1:T(8,128)(2,1)S(1)} %copy.96), channel_id=1, replica_groups=mesh['lat'=16,'lon'=2] {'lon'}, dimensions={1} | all-to-all | bytes 16220160 | tf_op jit(solution)/shard_map/all_to_all | solution.py:149
  879.5 10.9 %convert_bitcast_fusion = f32[22,720,2,128]{3,0,1,2:T(8,128)} fusion(bf16[22,2,720,128]{3,0,2,1:T(8,128)(2,1)} %bitcast.349), kind=kLoop, calls=%fused_computation.309 | loop fusion | flops 4055040 | bytes 24330240 | tf_op jit(solution)/shard_map/convert_element_type | solution.py:150
  890.4 23.6 %copy.97 = f32[22,720,2,128]{3,2,1,0:T(2,128)} copy(f32[22,720,2,128]{3,0,1,2:T(8,128)} %convert_bitcast_fusion) | data formatting | bytes 32440320 | tf_op jit(solution)/shard_map/convert_element_type | solution.py:150
  914.0 20.9 %reshape.1191 = f32[22,720,256]{2,1,0:T(8,128)} reshape(f32[22,720,2,128]{3,2,1,0:T(2,128)} %copy.97) | data formatting | bytes 32440320 | tf_op jit(solution)/shard_map/convert_element_type | solution.py:150
  934.9 11.7 %add_convert_fusion = bf16[22,720,256]{2,1,0:T(8,128)(2,1)} fusion(f32[22,720,256]{2,1,0:T(8,128)} %reshape.1191, bf16[22,720,256]{2,1,0:T(8,128)(2,1)} %param.6), kind=kLoop, calls=%fused_computation.310 | loop fusion | flops 12165120 | bytes 32440320 | tf_op jit(solution)/shard_map/convert_element_type | solution.py:150
  (348 shorter events, 68.3 us)
Async XLA Ops:
  20.0 110.3 %all-to-all-start = ((bf16[22,720,256]{1,0,2:T(8,128)(2,1)}), bf16[22,720,256]{1,0,2:T(8,128)(2,1)}, u32[]{:S(2)}, u32[]{:S(2)}) async-start(bf16[22,720,256]{1,0,2:T(8,128)(2,1)} %copy.82), calls=%async_computation | async-start | bytes 18874368 | tf_op jit(solution)/shard_map/all_to_all | solution.py:114
  152.8 7.4 copy-start.1
  152.8 7.4 copy-start.4
  152.8 211.4 %all-to-all-start.1 = ((bf16[22,384,128]{2,0,1:T(8,128)(2,1)}), bf16[22,384,128]{2,0,1:T(8,128)(2,1)}, u32[]{:S(2)}, u32[]{:S(2)}) async-start(bf16[22,384,128]{2,0,1:T(8,128)(2,1)} %copy.85), calls=%async_computation.1 | async-start | bytes 4718592 | tf_op jit(solution)/shard_map/all_to_all | solution.py:125
  160.2 453.4 %all-gather.3.cloned.1.call-start = ((), (), s32[]{:S(2)}) async-start(), calls=%async_computation.7 | async-start | bytes 4718592 | tf_op jit(solution)/shard_map/all_gather | solution.py:133
  382.3 245.4 %all-gather.5.cloned.1.call-start = ((), (), s32[]{:S(2)}) async-start(), calls=%async_computation.8 | async-start | bytes 13369344 | tf_op jit(solution)/shard_map/all_gather | solution.py:134
  395.9 132.1 %all-to-all-start.4 = ((bf16[22,720,256]{1,0,2:T(8,128)(2,1)}), bf16[22,720,256]{1,0,2:T(8,128)(2,1)}, u32[]{:S(2)}, u32[]{:S(2)}) async-start(bf16[22,720,256]{1,0,2:T(8,128)(2,1)} %copy.98), calls=%async_computation.4 | async-start | bytes 18874368 | tf_op jit(solution)/shard_map/all_to_all | solution.py:113
  403.3 543.2 %reduce-scatter.2.cloned.1.call-start = ((), (), s32[]{:S(2)}) async-start(), calls=%async_computation.9 | async-start | bytes 26738688 | tf_op jit(solution)/shard_map/reduce_scatter | solution.py:141
  405.7 134.4 %copy-start.2 = (bf16[1440,384]{0,1:T(8,128)(2,1)}, bf16[1440,384]{0,1:T(8,128)(2,1)S(1)}, u32[]{:S(2)}) copy-start(bf16[1440,384]{0,1:T(8,128)(2,1)S(1)} %convert_element_type.264) | copy-start | bytes 3317764
  627.6 1.9 copy-start
  747.8 1.3 copy-start.3
Sparse Core Ops, SparseCore 0:
  382.4 64.9 all-gather.2
  449.7 99.1 all-gather.4
  627.8 279.5 reduce-scatter.1
where the time goes:
time: 973 us; the launch traced here: 954 us
  blocking collectives  257 us (26%)
  waiting for transfers between devices  217 us (22%)
  local copies, waits for them, and re-layouts  171 us (18%)
  loops' own time  157 us (16%)
  other arithmetic  59.7 us (6%)
  matrix products  55 us (6%)
  starting transfers between devices  22.2 us (2%)
  between operations  14.4 us (1%)
    another operation x1, loops' own time, legendre_table(): _, blocks = lax.scan(advance_block, initial, starts)  157 us
    all_to_all x1, waiting for transfers between devices, local(): lax.all_to_all(grid_input, 'lon', split_axis=2, concat_axis=1, tiled=True)  122 us
    all_to_all x1, blocking collectives, local(): lax.all_to_all(grid_back, 'lon', split_axis=1, concat_axis=2, tiled=True)  102 us
    all_to_all x1, blocking collectives, local(): lax.all_to_all(back_rows, 'lat', split_axis=0, concat_axis=1, tiled=True)  96.7 us
    all_to_all x1, waiting for transfers between devices, local(): lax.all_to_all(cotangent, 'lon', split_axis=2, concat_axis=1, tiled=True)  94.4 us
    all_to_all x1, blocking collectives, local(): lax.all_to_all(spec_x, 'lat', split_axis=1, concat_axis=0, tiled=True)  58.5 us
    convert_element_type x2, local copies, waits for them, and re-layouts, local(): grid_local.astype(jnp.float32)  44.5 us
    unnamed x12, local copies, waits for them, and re-layouts  28.2 us
  transfers between devices with their start and end apart: 6, of which 2 were waited for; matrix products, arithmetic and copies ran while one was open for 24% of the time, Pallas kernels for 0%

commit v1 on v0

v1 whole, which is shorter than its diff:
```python
import math

import jax
import jax.numpy as jnp
from jax import lax
from jax.experimental import pallas as pl
from jax.experimental.pallas import tpu as pltpu
from jax.sharding import PartitionSpec as P


def quadrature(count_lat):
    colatitude = (jnp.arange(count_lat, dtype=jnp.float32) + 0.5) * (math.pi / count_lat)
    return math.pi / count_lat * jnp.sin(colatitude)


BLOCK = 16


def legendre_kernel(order_ref, cosine_ref, start_ref, out_ref, rows_ref):
    order = order_ref[...]
    cosine = cosine_ref[...]
    first_scale = jnp.sqrt(2.0 * order + 3.0)

    def advance(degree, carried):
        previous, earlier, scale_log = carried
        growth = jnp.sqrt(
            (4.0 * degree * degree - 1.0) / jnp.maximum(degree * degree - order * order, 1.0)
        )
        below = (degree - 1.0) * (degree - 1.0)
        shrink = jnp.sqrt(
            jnp.maximum(below - order * order, 0.0) / jnp.maximum(4.0 * below - 1.0, 1.0)
        )
        growth = jnp.where(degree == order + 1.0, first_scale, growth)
        growth = jnp.where(degree > order, growth, 0.0)
        current = growth * (cosine * previous - shrink * earlier)
        current = jnp.where(degree == order, 1.0, current)
        oversized = jnp.abs(current) > 10000000000.0
        factor = jnp.where(oversized, 1e-10, 1.0)
        scale_log = scale_log + jnp.where(oversized, math.log(10000000000.0), 0.0)
        current = current * factor
        return (current, previous * factor, scale_log), current * jnp.exp(scale_log)

    def block(index, carried):
        base = index * BLOCK
        for step in range(BLOCK):
            degree = (base + step).astype(jnp.float32)
            carried, value = advance(degree, carried)
            rows_ref[:, step, :] = value
        out_ref[:, pl.ds(pl.multiple_of(base, BLOCK), BLOCK), :] = rows_ref[...].astype(
            jnp.bfloat16
        )
        return carried

    zero = jnp.zeros(start_ref.shape, jnp.float32)
    lax.fori_loop(0, out_ref.shape[1] // BLOCK, block, (zero, zero, start_ref[...]))


def legendre_table(order_ids, count_lat, degrees, order_cap):
    colatitude = (jnp.arange(count_lat, dtype=jnp.float32) + 0.5) * (math.pi / count_lat)
    cosine = jnp.cos(colatitude)[None, :]
    sine_row = jnp.sin(colatitude)[None, :]
    order_value = order_ids.astype(jnp.float32)[:, None]
    counter = jnp.arange(1, order_cap + 1, dtype=jnp.float32)[None, :]
    log_terms = jnp.where(counter <= order_value, jnp.log1p(0.5 / counter), 0.0)
    log_start = (
        0.5 * math.log(0.5)
        + 0.5 * jnp.sum(log_terms, axis=1, keepdims=True)
        + order_value * jnp.log(sine_row)
    )
    orders = order_ids.shape[0]
    return pl.pallas_call(
        legendre_kernel,
        out_shape=jax.ShapeDtypeStruct((orders, degrees, count_lat), jnp.bfloat16),
        in_specs=[pl.BlockSpec(memory_space=pltpu.VMEM)] * 3,
        out_specs=pl.BlockSpec(memory_space=pltpu.VMEM),
        scratch_shapes=[pltpu.VMEM((orders, BLOCK, count_lat), jnp.float32)],
        compiler_params=pltpu.CompilerParams(vmem_limit_bytes=48 * 1024 * 1024),
    )(order_value, cosine, log_start)


def fourier_tables(order_ids, first, points_held, count_lon):
    points = first + jnp.arange(points_held, dtype=jnp.int32)
    phase_index = points[:, None] * order_ids[None, :] % count_lon
    angles = phase_index.astype(jnp.float32) * (2.0 * math.pi / count_lon)
    forward = jnp.stack([jnp.cos(angles), -jnp.sin(angles)], axis=2).reshape(
        points_held, 2 * order_ids.shape[0]
    )
    factor = jnp.where(order_ids == 0, 1.0, 2.0).astype(jnp.float32) / count_lon
    backward = forward * jnp.repeat(factor, 2)[None, :]
    return (forward.astype(jnp.bfloat16), backward.astype(jnp.bfloat16))


def swap(block, axis):
    return lax.all_to_all(block, axis, split_axis=0, concat_axis=0, tiled=True)


def partial_spectrum(field, table, scale, lon_count):
    rows, _, channels = field.shape
    part = jnp.einsum("jkc,kq->jqc", field, table, preferred_element_type=jnp.float32)
    if scale is not None:
        part = part * scale[:, None, None]
    part = part.astype(jnp.bfloat16).reshape(rows, -1, lon_count, channels // lon_count)
    return part.transpose(2, 1, 0, 3)


def local(grid_input, cotangent, mixing):
    lat_count = lax.axis_size("lat")
    lon_count = lax.axis_size("lon")
    lat_rows, lon_rows, channels = grid_input.shape
    count_lat = lat_rows * lat_count
    count_lon = lon_rows * lon_count
    per_dev = mixing.shape[0]
    order_total = per_dev * lat_count
    block_ch = channels // lon_count
    lat_pos = lax.axis_index("lat")
    lon_pos = lax.axis_index("lon")
    slot_ids = jnp.arange(order_total, dtype=jnp.int32)
    forward, backward = fourier_tables(slot_ids, lon_pos * lon_rows, lon_rows, count_lon)
    weights = quadrature(count_lat)
    own_weights = lax.dynamic_slice_in_dim(weights, lat_pos * lat_rows, lat_rows)
    own_orders = lat_pos * per_dev + jnp.arange(per_dev, dtype=jnp.int32)
    legendre = legendre_table(own_orders, count_lat, order_total, order_total)

    def analyse(part):
        full = swap(part, "lon").astype(jnp.float32).sum(0).astype(jnp.bfloat16)
        full = full.reshape(lat_count, per_dev, 2, lat_rows, block_ch)
        rows = swap(full, "lat")
        rows = rows.transpose(1, 0, 3, 2, 4).reshape(per_dev, count_lat, 2 * block_ch)
        out = jnp.einsum("mlj,mjc->mlc", legendre, rows, preferred_element_type=jnp.float32)
        out = out.astype(jnp.bfloat16).reshape(per_dev, lat_count, per_dev, 2, block_ch)
        out = swap(out.transpose(1, 2, 0, 3, 4), "lat")
        return out.transpose(1, 0, 2, 3, 4).reshape(per_dev, 2 * order_total, block_ch)

    adjoint = analyse(partial_spectrum(cotangent, backward, None, lon_count))
    full_adjoint = lax.all_gather(adjoint, "lon", axis=0)
    full_adjoint = full_adjoint.transpose(1, 2, 0, 3).reshape(per_dev, 2 * order_total, channels)
    mixed = jnp.einsum(
        "lqc,lic->lqi", full_adjoint, mixing, preferred_element_type=jnp.float32
    ).astype(jnp.bfloat16)
    mixed = mixed.reshape(per_dev, lat_count, per_dev, 2, block_ch).transpose(1, 0, 2, 3, 4)
    mixed = swap(mixed, "lat").transpose(2, 0, 1, 3, 4)
    mixed = mixed.reshape(per_dev, order_total, 2 * block_ch)
    back = jnp.einsum("mlj,mlc->mjc", legendre, mixed, preferred_element_type=jnp.float32)
    back = (back * weights[None, :, None]).astype(jnp.bfloat16)
    back = back.reshape(per_dev, lat_count, lat_rows, 2, block_ch).transpose(1, 2, 0, 3, 4)
    back = swap(back, "lat").transpose(1, 0, 2, 3, 4).reshape(lat_rows, 2 * order_total, block_ch)
    back = lax.all_gather(back, "lon", axis=0)
    back = back.transpose(1, 2, 0, 3).reshape(lat_rows, 2 * order_total, channels)
    grid_back = jnp.einsum("jqc,kq->jkc", back, forward, preferred_element_type=jnp.float32)
    grid_back = grid_back.astype(jnp.bfloat16).astype(jnp.float32)
    input_grad = (cotangent.astype(jnp.float32) + grid_back).astype(jnp.bfloat16)
    coefficients = analyse(partial_spectrum(grid_input, forward, own_weights, lon_count))
    weight_grad = jnp.einsum(
        "lqi,lqc->lic", coefficients, full_adjoint, preferred_element_type=jnp.float32
    )
    return (input_grad, weight_grad)


def solution(mesh):
    in_specs = (P("lat", "lon", None), P("lat", "lon", None), P("lat", "lon", None))
    out_specs = (P("lat", "lon", None), P("lat", "lon", None))
    return jax.shard_map(local, mesh=mesh, in_specs=in_specs, out_specs=out_specs, check_vma=False)
```

time: 973 us -> 518 us (0.53)
  blocking collectives: 257 us -> 85 us
  loops' own time: 157 us -> 0 us
  local copies, waits for them, and re-layouts: 171 us -> 84.7 us
  other arithmetic: 59.7 us -> 13.1 us
  starting transfers between devices: 22.2 us -> 38.1 us
    all_to_all x3 -> x2, blocking collectives: 257 us -> 85 us  [swap(): return lax.all_to_all(block, axis, split_axis=0, concat_axis=0, tiled=True)]
    another operation x1 -> x0, loops' own time: 157 us -> none  [legendre_table(): _, blocks = lax.scan(advance_block, initial, starts)]
    convert_element_type x7 -> x0, local copies, waits for them, and re-layouts: 76.6 us -> none  [the longest x2 44.5 us: local(): grid_local.astype(jnp.float32)]
    reshape x7 -> x16, local copies, waits for them, and re-layouts: 16.3 us -> 53 us  [the longest x2 11.8 us: analyse(): rows.transpose(1, 0, 3, 2, 4).reshape(per_dev, count_lat, 2 * block_ch)]
    all_gather x2, waiting for transfers between devices: 0.04 us -> 35.9 us  [the longest x1 35.9 us: local(): full_adjoint = lax.all_gather(adjoint, 'lon', axis=0)]
    all_to_all x3 -> x6, waiting for transfers between devices: 217 us -> 185 us  [swap(): return lax.all_to_all(block, axis, split_axis=0, concat_axis=0, tiled=True)]
    all_to_all x5 -> x0, local copies, waits for them, and re-layouts: 28.8 us -> none  [the longest x1 12.5 us: local(): lax.all_to_all(cotangent, 'lon', split_axis=2, concat_axis=1, tiled=True)]
    unnamed x12 -> x8, local copies, waits for them, and re-layouts: 28.2 us -> 0.02 us
  transfers between devices with their start and end apart: 6 -> 8, of which waited for: 2 -> 7; matrix products, arithmetic and copies ran while one was open for 24% -> 16% of each run, Pallas kernels for 0% -> 1%
where the time goes in v1:
time: 518 us; the launch traced here: 507 us
  waiting for transfers between devices  221 us (43%)
  blocking collectives  85 us (16%)
  local copies, waits for them, and re-layouts  84.7 us (16%)
  matrix products  45.6 us (9%)
  starting transfers between devices  38.1 us (7%)
  between operations  14.7 us (3%)
  other arithmetic  13.1 us (3%)
  Pallas kernels  5.29 us (1%)
    all_to_all x6, waiting for transfers between devices, swap(): return lax.all_to_all(block, axis, split_axis=0, concat_axis=0, tiled=True)  185 us
    all_to_all x2, blocking collectives, swap(): return lax.all_to_all(block, axis, split_axis=0, concat_axis=0, tiled=True)  85 us
    all_to_all x6, starting transfers between devices, swap(): return lax.all_to_all(block, axis, split_axis=0, concat_axis=0, tiled=True)  37.8 us
    all_gather x1, waiting for transfers between devices, local(): full_adjoint = lax.all_gather(adjoint, 'lon', axis=0)  35.9 us
    dot_general x2, matrix products, partial_spectrum(): jnp.einsum('jkc,kq->jqc', field, table, preferred_element_type=jnp.float32)  18.9 us
    reshape x2, local copies, waits for them, and re-layouts, analyse(): rows.transpose(1, 0, 3, 2, 4).reshape(per_dev, count_lat, 2 * block_ch)  11.8 us
    dot_general x1, matrix products, local(): jnp.einsum('jqc,kq->jkc', back, forward, preferred_element_type=jnp.float32)  10.4 us
  transfers between devices with their start and end apart: 8, of which 7 were waited for; matrix products, arithmetic and copies ran while one was open for 16% of the time, Pallas kernels for 1%

profile of v1, /device:TPU:27, one launch (start us, length us, event | category | flops | bytes accessed | tf_op | source)
XLA Modules:
  0.0 507.4 jit_solution(2552461353623330462)
XLA Ops:
  12.8 8.4 %convolution_convert_fusion = bf16[384,22,256]{0,2,1:T(8,128)(2,1)S(1)} fusion(bf16[22,720,256]{2,1,0:T(8,128)(2,1)} %param.4, f32[720,384]{0,1:T(8,128)} %reshape.201, f32[384]{0:T(512)S(1)} %mul.144), kind=kOutput, calls=%fused_computation.8 | convolution fusion | flops 3116986368 | bytes 13542912 | tf_op jit(solution)/shard_map/jkc,kq->jqc/dot_general | solution.py:99
  21.9 52.3 %all_to_all.40 = bf16[2,384,22,128]{1,3,2,0:T(8,128)(2,1)} all-to-all(bf16[2,384,22,128]{1,3,2,0:T(8,128)(2,1)S(1)} %bitcast.87), channel_id=1, replica_groups=mesh['lat'=16,'lon'=2] {'lon'}, dimensions={0} | all-to-all | bytes 8650752 | tf_op jit(solution)/shard_map/all_to_all | solution.py:94
  74.3 5.0 reduce_sum.34
  79.3 4.1 copy.72
  83.4 4.4 copy.73
  87.9 7.2 %all-to-all-start.1 = ((bf16[16,12,2,22,128]{4,2,1,3,0:T(2,128)(2,1)}), bf16[16,12,2,22,128]{4,2,1,3,0:T(2,128)(2,1)}, u32[]{:S(2)}, u32[]{:S(2)}) async-start(bf16[16,12,2,22,128]{4,2,1,3,0:T(2,128)(2,1)} %copy.73), calls=%async_computation.1 | async-start | bytes 4325376 | tf_op jit(solution)/shard_map/all_to_all | solution.py:94
  95.6 5.3 %shard_map.50 = bf16[12,192,352]{2,1,0:T(8,128)(2,1)S(1)} custom-call(f32[12,1]{1,0:T(8,128)S(1)} %add_convert_fusion.order_ref, f32[1,352]{1,0:T(1,128)S(1)} %multiply_cosine_fusion.cosine_ref, f32[12,352]{1,0:T(8,128)S(1)} %multiply_add_fusion.start_ref), custom_call_target="tpu_custom_call" | custom-call | tf_op jit(solution)/shard_map/pallas_call | solution.py:71
  100.9 42.2 %all-to-all-done.1 = bf16[16,12,2,22,128]{4,2,1,3,0:T(2,128)(2,1)} async-done(((bf16[16,12,2,22,128]{4,2,1,3,0:T(2,128)(2,1)}), bf16[16,12,2,22,128]{4,2,1,3,0:T(2,128)(2,1)}, u32[]{:S(2)}, u32[]{:S(2)}) %all-to-all-start.1) | async-done | bytes 2162720 | tf_op jit(solution)/shard_map/all_to_all | solution.py:94
  143.0 4.8 copy.74
  147.8 5.9 %reshape.204 = bf16[12,352,256]{2,1,0:T(8,128)(2,1)} reshape(bf16[12,16,22,2,128]{4,3,2,1,0:T(2,128)(2,1)} %copy.74) | data formatting | bytes 4325376 | tf_op jit(solution)/shard_map/reshape | solution.py:128
  162.8 32.6 %all_to_all.41 = bf16[16,12,12,2,128]{4,3,2,1,0:T(2,128)(2,1)S(1)} all-to-all(bf16[16,12,12,2,128]{4,3,2,1,0:T(2,128)(2,1)S(1)} %bitcast.97), channel_id=1, replica_groups=mesh['lat'=16,'lon'=2] {'lat'}, dimensions={0} | all-to-all | bytes 2359296 | tf_op jit(solution)/shard_map/all_to_all | solution.py:94
  197.5 35.9 %all-gather.3.cloned.1.call-done = bf16[2,12,384,128]{3,2,1,0:T(8,128)(2,1)} async-done(((bf16[1,12,384,128]{3,2,1,0:T(8,128)(2,1)}), bf16[2,12,384,128]{3,2,1,0:T(8,128)(2,1)}) %all-gather.3.cloned.1.call-update) | async-done | bytes 2359312 | tf_op jit(solution)/shard_map/all_gather | solution.py:135
  237.7 6.3 %all-to-all-start.3 = ((bf16[16,12,12,2,128]{4,3,2,1,0:T(2,128)(2,1)}), bf16[16,12,12,2,128]{4,3,2,1,0:T(2,128)(2,1)}, u32[]{:S(2)}, u32[]{:S(2)}) async-start(bf16[16,12,12,2,128]{4,3,2,1,0:T(2,128)(2,1)} %bitcast.93), calls=%async_computation.3 | async-start | bytes 2359296 | tf_op jit(solution)/shard_map/all_to_all | solution.py:94
  245.7 10.4 %multiply_convert_fusion = bf16[384,22,256]{0,2,1:T(8,128)(2,1)S(1)} fusion(f32[22]{0:T(128)S(1)} %dynamic_slice.3, bf16[22,720,256]{2,1,0:T(8,128)(2,1)} %param.3, bf16[720,384]{1,0:T(8,128)(2,1)S(1)} %copy.84), kind=kOutput, calls=%fused_computation.2 | convolution fusion | flops 3118596096 | bytes 12988504 | tf_op jit(solution)/shard_map/jkc,kq->jqc/dot_general | solution.py:99
  258.8 12.1 %all-to-all-done.3 = bf16[16,12,12,2,128]{4,3,2,1,0:T(2,128)(2,1)} async-done(((bf16[16,12,12,2,128]{4,3,2,1,0:T(2,128)(2,1)}), bf16[16,12,12,2,128]{4,3,2,1,0:T(2,128)(2,1)}, u32[]{:S(2)}, u32[]{:S(2)}) %all-to-all-start.3) | async-done | bytes 1179680 | tf_op jit(solution)/shard_map/all_to_all | solution.py:94
  270.8 5.9 %all-to-all-start.5 = ((bf16[2,384,22,128]{1,3,2,0:T(8,128)(2,1)}), bf16[2,384,22,128]{1,3,2,0:T(8,128)(2,1)}, u32[]{:S(2)}, u32[]{:S(2)}) async-start(bf16[2,384,22,128]{1,3,2,0:T(8,128)(2,1)} %bitcast.86), calls=%async_computation.5 | async-start | bytes 8650752 | tf_op jit(solution)/shard_map/all_to_all | solution.py:94
  287.5 5.1 %reshape.209 = bf16[12,16,22,2,128]{4,3,2,1,0:T(2,128)(2,1)} reshape(bf16[12,352,256]{2,1,0:T(8,128)(2,1)} %multiply_convert_fusion.1) | data formatting | bytes 4325376 | tf_op jit(solution)/shard_map/reshape | solution.py:145
  292.7 4.4 copy.124
  297.1 28.3 %all-to-all-done.5 = bf16[2,384,22,128]{1,3,2,0:T(8,128)(2,1)} async-done(((bf16[2,384,22,128]{1,3,2,0:T(8,128)(2,1)}), bf16[2,384,22,128]{1,3,2,0:T(8,128)(2,1)}, u32[]{:S(2)}, u32[]{:S(2)}) %all-to-all-start.5) | async-done | bytes 4325408 | tf_op jit(solution)/shard_map/all_to_all | solution.py:94
  325.4 6.7 %all-to-all-start.4 = ((bf16[16,22,12,2,128]{4,3,2,1,0:T(2,128)(2,1)}), bf16[16,22,12,2,128]{4,3,2,1,0:T(2,128)(2,1)}, u32[]{:S(2)}, u32[]{:S(2)}) async-start(bf16[16,22,12,2,128]{4,3,2,1,0:T(2,128)(2,1)} %bitcast.89), calls=%async_computation.4 | async-start | bytes 4325376 | tf_op jit(solution)/shard_map/all_to_all | solution.py:94
  332.1 5.0 reduce_sum.35
  337.1 4.1 copy.87
  341.2 4.5 copy.88
  345.8 34.3 %all-to-all-done.4 = bf16[16,22,12,2,128]{4,3,2,1,0:T(2,128)(2,1)} async-done(((bf16[16,22,12,2,128]{4,3,2,1,0:T(2,128)(2,1)}), bf16[16,22,12,2,128]{4,3,2,1,0:T(2,128)(2,1)}, u32[]{:S(2)}, u32[]{:S(2)}) %all-to-all-start.4) | async-done | bytes 2162720 | tf_op jit(solution)/shard_map/all_to_all | solution.py:94
  380.1 5.9 %all-to-all-start.6 = ((bf16[16,12,2,22,128]{4,2,1,3,0:T(2,128)(2,1)}), bf16[16,12,2,22,128]{4,2,1,3,0:T(2,128)(2,1)}, u32[]{:S(2)}, u32[]{:S(2)}) async-start(bf16[16,12,2,22,128]{4,2,1,3,0:T(2,128)(2,1)} %copy.88), calls=%async_computation.6 | async-start | bytes 4325376 | tf_op jit(solution)/shard_map/all_to_all | solution.py:94
  386.2 5.1 %copy.81 = bf16[22,16,12,2,128]{4,3,2,1,0:T(2,128)(2,1)} copy(bf16[22,16,12,2,128]{4,3,2,0,1:T(2,128)(2,1)} %bitcast.15) | data formatting | bytes 4325376 | tf_op jit(solution)/shard_map/transpose | solution.py:146
  391.4 42.5 %all-to-all-done.6 = bf16[16,12,2,22,128]{4,2,1,3,0:T(2,128)(2,1)} async-done(((bf16[16,12,2,22,128]{4,2,1,3,0:T(2,128)(2,1)}), bf16[16,12,2,22,128]{4,2,1,3,0:T(2,128)(2,1)}, u32[]{:S(2)}, u32[]{:S(2)}) %all-to-all-start.6) | async-done | bytes 2162720 | tf_op jit(solution)/shard_map/all_to_all | solution.py:94
  433.9 4.9 copy.89
  438.8 5.9 %reshape.213 = bf16[12,352,256]{2,1,0:T(8,128)(2,1)} reshape(bf16[12,16,22,2,128]{4,3,2,1,0:T(2,128)(2,1)} %copy.89) | data formatting | bytes 4325376 | tf_op jit(solution)/shard_map/reshape | solution.py:128
  452.7 5.9 %all-to-all-start.7 = ((bf16[16,12,12,2,128]{4,3,2,1,0:T(2,128)(2,1)}), bf16[16,12,12,2,128]{4,3,2,1,0:T(2,128)(2,1)S(1)}, u32[]{:S(2)}, u32[]{:S(2)}) async-start(bf16[16,12,12,2,128]{4,3,2,1,0:T(2,128)(2,1)} %bitcast.95), calls=%async_computation.7 | async-start | bytes 2359296 | tf_op jit(solution)/shard_map/all_to_all | solution.py:94
  459.7 25.6 %all-to-all-done.7 = bf16[16,12,12,2,128]{4,3,2,1,0:T(2,128)(2,1)S(1)} async-done(((bf16[16,12,12,2,128]{4,3,2,1,0:T(2,128)(2,1)}), bf16[16,12,12,2,128]{4,3,2,1,0:T(2,128)(2,1)S(1)}, u32[]{:S(2)}, u32[]{:S(2)}) %all-to-all-start.7) | async-done | bytes 1179680 | tf_op jit(solution)/shard_map/all_to_all | solution.py:94
  489.8 10.4 %fusion = bf16[22,720,256]{2,1,0:T(8,128)(2,1)} fusion(bf16[22,720,256]{2,1,0:T(8,128)(2,1)} %param.4, bf16[720,384]{0,1:T(8,128)(2,1)S(1)} %convert_element_type.91, bf16[2,22,384,128]{3,2,1,0:T(8,128)(2,1)} %all-gather.5.cloned.1.call-done), kind=kOutput, calls=%fused_computation.1 | convolution fusion | flops 3134545920 | bytes 21098496 | tf_op jit(solution)/shard_map/jqc,kq->jkc/dot_general | solution.py:149
  (51 shorter events, 51.1 us)
Async XLA Ops:
  7.2 226.2 %copy-start = (bf16[12,128,256]{2,1,0:T(8,128)(2,1)S(1)}, bf16[12,128,256]{2,1,0:T(8,128)(2,1)}, u32[]{:S(2)}) copy-start(bf16[12,128,256]{2,1,0:T(8,128)(2,1)} %param.5) | copy-start | bytes 2359300
  9.7 1.0 copy-start.2
  87.9 55.2 %all-to-all-start.1 = ((bf16[16,12,2,22,128]{4,2,1,3,0:T(2,128)(2,1)}), bf16[16,12,2,22,128]{4,2,1,3,0:T(2,128)(2,1)}, u32[]{:S(2)}, u32[]{:S(2)}) async-start(bf16[16,12,2,22,128]{4,2,1,3,0:T(2,128)(2,1)} %copy.73), calls=%async_computation.1 | async-start | bytes 4325376 | tf_op jit(solution)/shard_map/all_to_all | solution.py:94
  95.1 138.3 %all-gather.3.cloned.1.call-start = ((), (), s32[]{:S(2)}) async-start(), calls=%async_computation.8 | async-start | bytes 3538944 | tf_op jit(solution)/shard_map/all_gather | solution.py:135
  237.7 33.2 %all-to-all-start.3 = ((bf16[16,12,12,2,128]{4,3,2,1,0:T(2,128)(2,1)}), bf16[16,12,12,2,128]{4,3,2,1,0:T(2,128)(2,1)}, u32[]{:S(2)}, u32[]{:S(2)}) async-start(bf16[16,12,12,2,128]{4,3,2,1,0:T(2,128)(2,1)} %bitcast.93), calls=%async_computation.3 | async-start | bytes 2359296 | tf_op jit(solution)/shard_map/all_to_all | solution.py:94
  270.8 54.6 %all-to-all-start.5 = ((bf16[2,384,22,128]{1,3,2,0:T(8,128)(2,1)}), bf16[2,384,22,128]{1,3,2,0:T(8,128)(2,1)}, u32[]{:S(2)}, u32[]{:S(2)}) async-start(bf16[2,384,22,128]{1,3,2,0:T(8,128)(2,1)} %bitcast.86), calls=%async_computation.5 | async-start | bytes 8650752 | tf_op jit(solution)/shard_map/all_to_all | solution.py:94
  325.4 54.6 %all-to-all-start.4 = ((bf16[16,22,12,2,128]{4,3,2,1,0:T(2,128)(2,1)}), bf16[16,22,12,2,128]{4,3,2,1,0:T(2,128)(2,1)}, u32[]{:S(2)}, u32[]{:S(2)}) async-start(bf16[16,22,12,2,128]{4,3,2,1,0:T(2,128)(2,1)} %bitcast.89), calls=%async_computation.4 | async-start | bytes 4325376 | tf_op jit(solution)/shard_map/all_to_all | solution.py:94
  380.1 53.8 %all-to-all-start.6 = ((bf16[16,12,2,22,128]{4,2,1,3,0:T(2,128)(2,1)}), bf16[16,12,2,22,128]{4,2,1,3,0:T(2,128)(2,1)}, u32[]{:S(2)}, u32[]{:S(2)}) async-start(bf16[16,12,2,22,128]{4,2,1,3,0:T(2,128)(2,1)} %copy.88), calls=%async_computation.6 | async-start | bytes 4325376 | tf_op jit(solution)/shard_map/all_to_all | solution.py:94
  385.9 103.8 %all-gather.5.cloned.1.call-start = ((), (), s32[]{:S(2)}) async-start(), calls=%async_computation.9 | async-start | bytes 6488064 | tf_op jit(solution)/shard_map/all_gather | solution.py:147
  450.8 7.7 %copy-start.3 = (f32[720,192,1]{0,1,2:T(8,128)S(1)}, f32[720,192,1]{0,1,2:T(8,128)}, u32[]{:S(2)}) copy-start(f32[720,192,1]{0,1,2:T(8,128)} %copy-done.2) | copy-start | bytes 1658884
  452.7 32.6 %all-to-all-start.7 = ((bf16[16,12,12,2,128]{4,3,2,1,0:T(2,128)(2,1)}), bf16[16,12,12,2,128]{4,3,2,1,0:T(2,128)(2,1)S(1)}, u32[]{:S(2)}, u32[]{:S(2)}) async-start(bf16[16,12,12,2,128]{4,3,2,1,0:T(2,128)(2,1)} %bitcast.95), calls=%async_computation.7 | async-start | bytes 2359296 | tf_op jit(solution)/shard_map/all_to_all | solution.py:94
  489.8 10.4 %copy-start.1 = (bf16[12,128,256]{2,1,0:T(8,128)(2,1)S(1)}, bf16[12,128,256]{2,1,0:T(8,128)(2,1)}, u32[]{:S(2)}) copy-start(bf16[12,128,256]{2,1,0:T(8,128)(2,1)} %param.5) | copy-start | bytes 2359300
Sparse Core Ops, SparseCore 0:
  197.6 35.7 all-gather.2
  391.5 57.9 all-gather.4

commit v2 on v1

--- a/solution.py
+++ b/solution.py
@@ -1,3 +1,4 @@
+import functools
 import math
 
 import jax
@@ -90,17 +91,323 @@
     return (forward.astype(jnp.bfloat16), backward.astype(jnp.bfloat16))
 
 
-def swap(block, axis):
-    return lax.all_to_all(block, axis, split_axis=0, concat_axis=0, tiled=True)
-
-
-def partial_spectrum(field, table, scale, lon_count):
-    rows, _, channels = field.shape
-    part = jnp.einsum("jkc,kq->jqc", field, table, preferred_element_type=jnp.float32)
-    if scale is not None:
-        part = part * scale[:, None, None]
-    part = part.astype(jnp.bfloat16).reshape(rows, -1, lon_count, channels // lon_count)
-    return part.transpose(2, 1, 0, 3)
+MESH = pl.DeviceIdType.MESH
+VMEM = pl.BlockSpec(memory_space=pltpu.VMEM)
+SMEM = pl.BlockSpec(memory_space=pltpu.SMEM)
+ANY = pl.BlockSpec(memory_space=pl.ANY)
+
+
+def limits(**more):
+    return pltpu.CompilerParams(vmem_limit_bytes=48 * 1024 * 1024, **more)
+
+
+def peer(axis, count, offset):
+    return lax.rem(lax.axis_index(axis) + offset + count, count)
+
+
+def swap_copy(source, target, sems, axis, count, offset):
+    there = peer(axis, count, offset)
+    return pltpu.make_async_remote_copy(
+        src_ref=source.at[there],
+        dst_ref=target.at[lax.axis_index(axis)],
+        send_sem=sems.at[0, offset],
+        recv_sem=sems.at[1, offset],
+        device_id={axis: there},
+        device_id_type=MESH,
+    )
+
+
+def spread_copy(target, slot, sems, offset, step, lon_count):
+    here = lax.axis_index("lon")
+    return pltpu.make_async_remote_copy(
+        src_ref=target.at[here, slot],
+        dst_ref=target.at[here, slot],
+        send_sem=sems.at[0, offset, step],
+        recv_sem=sems.at[1, offset, step],
+        device_id={"lon": peer("lon", lon_count, offset)},
+        device_id_type=MESH,
+    )
+
+
+def exchange_kernel(jobs, counts, *refs):
+    total = len(jobs)
+    sources, targets, sems = refs[:total], refs[total : 2 * total], refs[2 * total :]
+    lat_count, lon_count = counts["lat"], counts["lon"]
+    axes = [axis for axis in ("lon", "lat") if axis in jobs or "spread" in jobs]
+
+    barrier = pltpu.get_barrier_semaphore()
+    expected = 0
+    for axis in axes:
+
+        def greet(offset, carried, axis=axis):
+            there = peer(axis, counts[axis], offset)
+            pl.semaphore_signal(barrier, inc=1, device_id={axis: there}, device_id_type=MESH)
+            return carried
+
+        lax.fori_loop(1, counts[axis], greet, 0)
+        expected += counts[axis] - 1
+    pl.semaphore_wait(barrier, expected)
+
+    place = 0
+    plans = []
+    for kind, source, target in zip(jobs, sources, targets):
+        axis = "lat" if kind == "spread" else kind
+        landing = target.at[lax.axis_index("lon")] if kind == "spread" else target
+        own = pltpu.make_async_copy(
+            source.at[lax.axis_index(axis)], landing.at[lax.axis_index(axis)], sems[place]
+        )
+        plans.append((kind, axis, source, landing, target, own, sems[place + 1], sems[place + 2]))
+        place += 3
+    for kind, axis, source, landing, target, own, first, second in plans:
+
+        def start(offset, carried, plan=(source, landing, first, axis, counts[axis])):
+            swap_copy(*plan, offset).start()
+            return carried
+
+        lax.fori_loop(1, counts[axis], start, 0)
+        own.start()
+    for kind, axis, source, landing, target, own, first, second in plans:
+        own.wait()
+        if kind == "spread":
+            for ahead in range(1, lon_count):
+                spread_copy(target, peer("lat", lat_count, 0), second, ahead, 0, lon_count).start()
+
+        def arrive(offset, carried, plan=(source, landing, first, axis, counts[axis])):
+            swap_copy(*plan, offset).wait_recv()
+            return carried
+
+        def arrive_and_spread(offset, carried, target=target, second=second, arrive=arrive):
+            arrive(offset, carried)
+            slot = peer("lat", lat_count, -offset)
+            for ahead in range(1, lon_count):
+                spread_copy(target, slot, second, ahead, offset, lon_count).start()
+            return carried
+
+        lax.fori_loop(1, counts[axis], arrive_and_spread if kind == "spread" else arrive, 0)
+    for kind, axis, source, landing, target, own, first, second in plans:
+
+        def leave(offset, carried, plan=(source, landing, first, axis, counts[axis])):
+            swap_copy(*plan, offset).wait_send()
+            return carried
+
+        lax.fori_loop(1, counts[axis], leave, 0)
+        if kind == "spread":
+
+            def finish(offset, carried, target=target, second=second):
+                slot = peer("lat", lat_count, -offset)
+                for ahead in range(1, lon_count):
+                    copy = spread_copy(target, slot, second, ahead, offset, lon_count)
+                    copy.wait_send()
+                    copy.wait_recv()
+                return carried
+
+            lax.fori_loop(0, lat_count, finish, 0)
+
+
+def exchange(ident, *pairs):
+    counts = {"lat": lax.axis_size("lat"), "lon": lax.axis_size("lon")}
+    kinds = [kind for kind, _ in pairs]
+    arrays = [array for _, array in pairs]
+    shapes, scratch = [], []
+    for kind, array in pairs:
+        shape = (counts["lon"],) + array.shape if kind == "spread" else array.shape
+        shapes.append(jax.ShapeDtypeStruct(shape, array.dtype))
+        axis = "lat" if kind == "spread" else kind
+        scratch.append(pltpu.SemaphoreType.DMA)
+        scratch.append(pltpu.SemaphoreType.DMA((2, counts[axis])))
+        further = (2, counts["lon"], counts["lat"]) if kind == "spread" else (1,)
+        scratch.append(pltpu.SemaphoreType.DMA(further))
+    return pl.pallas_call(
+        functools.partial(exchange_kernel, kinds, counts),
+        out_shape=shapes,
+        in_specs=[ANY] * len(arrays),
+        out_specs=[ANY] * len(arrays),
+        scratch_shapes=scratch,
+        compiler_params=limits(collective_id=ident, has_side_effects=True),
+    )(*arrays)
+
+
+PAIR = 2
+
+
+def spectrum_kernel(lon_count, scale_ref, table_ref, field_ref, out_ref):
+    _, lat_count, depth, width = out_ref.shape
+    step = pl.program_id(0)
+    parts = []
+    for row in range(PAIR):
+        part = jnp.dot(table_ref[...], field_ref[row], preferred_element_type=jnp.float32)
+        parts.append(part * scale_ref[step * PAIR + row])
+    for owner in range(lon_count):
+        piece = [
+            part[:, owner * width : (owner + 1) * width].reshape(lat_count, depth // PAIR, width)
+            for part in parts
+        ]
+        out_ref[owner] = jnp.concatenate(piece, axis=1).astype(jnp.bfloat16)
+
+
+def partial_spectrum(field, table, scale, lat_count, lon_count):
+    rows, points, channels = field.shape
+    orders = table.shape[0] // lat_count
+    width = channels // lon_count
+    block = (lon_count, lat_count, PAIR * orders, width)
+    return pl.pallas_call(
+        functools.partial(spectrum_kernel, lon_count),
+        grid=(rows // PAIR,),
+        out_shape=jax.ShapeDtypeStruct(
+            (lon_count, lat_count, rows * orders, width), jnp.bfloat16
+        ),
+        in_specs=[
+            SMEM,
+            pl.BlockSpec(table.shape, lambda i: (0, 0)),
+            pl.BlockSpec((PAIR, points, channels), lambda i: (i, 0, 0)),
+        ],
+        out_specs=pl.BlockSpec(block, lambda i: (0, 0, i, 0)),
+        compiler_params=limits(),
+    )(scale, table, field)
+
+
+def transform_kernel(forward, legendre_ref, scale_ref, in_ref, out_ref, in_rows, out_rows):
+    orders, degrees, count_lat = legendre_ref.shape
+    taken, given = (count_lat, degrees) if forward else (degrees, count_lat)
+    width = in_ref.shape[1]
+    in_rows[...] = in_ref[...].astype(jnp.float32)
+    for order in range(orders):
+        piece = [in_rows[pl.ds(2 * order + r, taken, stride=2 * orders), :] for r in range(2)]
+        value = lax.dot_general(
+            legendre_ref[order],
+            jnp.concatenate(piece, axis=1).astype(jnp.bfloat16),
+            (((1 if forward else 0,), (0,)), ((), ())),
+            preferred_element_type=jnp.float32,
+        )
+        if not forward:
+            value = value * scale_ref[...]
+        for r in range(2):
+            out_rows[pl.ds(2 * order + r, given, stride=2 * orders), :] = value[
+                :, r * width : (r + 1) * width
+            ]
+    out_ref[...] = out_rows[...].astype(jnp.bfloat16)
+
+
+def transform(forward, legendre, scale, rows):
+    orders, degrees, count_lat = legendre.shape
+    height = 2 * orders * (degrees if forward else count_lat)
+    return pl.pallas_call(
+        functools.partial(transform_kernel, forward),
+        out_shape=jax.ShapeDtypeStruct((height, rows.shape[1]), jnp.bfloat16),
+        in_specs=[VMEM] * 3,
+        out_specs=VMEM,
+        scratch_shapes=[
+            pltpu.VMEM(rows.shape, jnp.float32),
+            pltpu.VMEM((height, rows.shape[1]), jnp.float32),
+        ],
+        compiler_params=limits(),
+    )(legendre, scale, rows)
+
+
+def degree_rows(ref, lead, pair, depth):
+    block = ref[lead + (slice(None), slice(pair * PAIR * depth, (pair + 1) * PAIR * depth))]
+    block = block.astype(jnp.float32)
+    count, _, width = block.shape
+    return [
+        block[:, i * depth : (i + 1) * depth].reshape(count * depth, width).astype(jnp.bfloat16)
+        for i in range(PAIR)
+    ]
+
+
+def all_channels(ref, pair, depth):
+    owners = [degree_rows(ref, (o,), pair, depth) for o in range(ref.shape[0])]
+    return [jnp.concatenate([rows[i] for rows in owners], axis=1) for i in range(PAIR)]
+
+
+def mix_kernel(adjoint_ref, mixing_ref, out_ref):
+    degrees, width = mixing_ref.shape[:2]
+    _, lat_count, height, _ = adjoint_ref.shape
+    depth = height // degrees
+    for pair in range(degrees // PAIR):
+        values = []
+        for i, full in enumerate(all_channels(adjoint_ref, pair, depth)):
+            value = lax.dot_general(
+                full,
+                mixing_ref[pair * PAIR + i],
+                (((1,), (1,)), ((), ())),
+                preferred_element_type=jnp.float32,
+            )
+            values.append(value.reshape(lat_count, depth, width))
+        out_ref[:, pair * PAIR * depth : (pair + 1) * PAIR * depth, :] = jnp.concatenate(
+            values, axis=1
+        ).astype(jnp.bfloat16)
+
+
+def mix(adjoint, mixing):
+    return pl.pallas_call(
+        mix_kernel,
+        out_shape=jax.ShapeDtypeStruct(adjoint.shape[1:], jnp.bfloat16),
+        in_specs=[VMEM] * 2,
+        out_specs=VMEM,
+        compiler_params=limits(),
+    )(adjoint, mixing)
+
+
+def weight_kernel(adjoint_ref, coefficient_ref, out_ref):
+    degrees = out_ref.shape[0]
+    depth = adjoint_ref.shape[2] // degrees
+    for pair in range(degrees // PAIR):
+        full = all_channels(adjoint_ref, pair, depth)
+        own = degree_rows(coefficient_ref, (), pair, depth)
+        for i in range(PAIR):
+            out_ref[pair * PAIR + i] = lax.dot_general(
+                own[i], full[i], (((0,), (0,)), ((), ())), preferred_element_type=jnp.float32
+            )
+
+
+def weight_gradient(adjoint, coefficients, degrees):
+    lon_count, _, _, width = adjoint.shape
+    return pl.pallas_call(
+        weight_kernel,
+        out_shape=jax.ShapeDtypeStruct((degrees, width, lon_count * width), jnp.float32),
+        in_specs=[VMEM] * 2,
+        out_specs=VMEM,
+        compiler_params=limits(),
+    )(adjoint, coefficients)
+
+
+def grid_kernel(table_ref, back_ref, field_ref, out_ref):
+    lon_count, lat_count, height, width = back_ref.shape
+    depth = height // PAIR
+    back = back_ref[...].astype(jnp.float32)
+    for row in range(PAIR):
+        piece = [
+            back[o, :, row * depth : (row + 1) * depth, :].reshape(lat_count * depth, width)
+            for o in range(lon_count)
+        ]
+        full = jnp.concatenate(piece, axis=1).astype(jnp.bfloat16)
+        value = jnp.dot(table_ref[...], full, preferred_element_type=jnp.float32)
+        value = value.astype(jnp.bfloat16).astype(jnp.float32)
+        out_ref[row] = (field_ref[row].astype(jnp.float32) + value).astype(jnp.bfloat16)
+
+
+def grid_gradient(table, back, field):
+    rows, points, channels = field.shape
+    lon_count, lat_count, height, width = back.shape
+    block = (PAIR, points, channels)
+    return pl.pallas_call(
+        grid_kernel,
+        grid=(rows // PAIR,),
+        out_shape=jax.ShapeDtypeStruct(field.shape, jnp.bfloat16),
+        in_specs=[
+            pl.BlockSpec(table.shape, lambda i: (0, 0)),
+            pl.BlockSpec(
+                (lon_count, lat_count, height // (rows // PAIR), width), lambda i: (0, 0, i, 0)
+            ),
+            pl.BlockSpec(block, lambda i: (i, 0, 0)),
+        ],
+        out_specs=pl.BlockSpec(block, lambda i: (i, 0, 0)),
+        compiler_params=limits(),
+    )(table, back, field)
+
+
+def add_parts(parts):
+    return jnp.sum(parts.astype(jnp.float32), axis=0).astype(jnp.bfloat16)
 
 
 def local(grid_input, cotangent, mixing):
@@ -120,39 +427,27 @@
     own_weights = lax.dynamic_slice_in_dim(weights, lat_pos * lat_rows, lat_rows)
     own_orders = lat_pos * per_dev + jnp.arange(per_dev, dtype=jnp.int32)
     legendre = legendre_table(own_orders, count_lat, order_total, order_total)
-
-    def analyse(part):
-        full = swap(part, "lon").astype(jnp.float32).sum(0).astype(jnp.bfloat16)
-        full = full.reshape(lat_count, per_dev, 2, lat_rows, block_ch)
-        rows = swap(full, "lat")
-        rows = rows.transpose(1, 0, 3, 2, 4).reshape(per_dev, count_lat, 2 * block_ch)
-        out = jnp.einsum("mlj,mjc->mlc", legendre, rows, preferred_element_type=jnp.float32)
-        out = out.astype(jnp.bfloat16).reshape(per_dev, lat_count, per_dev, 2, block_ch)
-        out = swap(out.transpose(1, 2, 0, 3, 4), "lat")
-        return out.transpose(1, 0, 2, 3, 4).reshape(per_dev, 2 * order_total, block_ch)
-
-    adjoint = analyse(partial_spectrum(cotangent, backward, None, lon_count))
-    full_adjoint = lax.all_gather(adjoint, "lon", axis=0)
-    full_adjoint = full_adjoint.transpose(1, 2, 0, 3).reshape(per_dev, 2 * order_total, channels)
-    mixed = jnp.einsum(
-        "lqc,lic->lqi", full_adjoint, mixing, preferred_element_type=jnp.float32
-    ).astype(jnp.bfloat16)
-    mixed = mixed.reshape(per_dev, lat_count, per_dev, 2, block_ch).transpose(1, 0, 2, 3, 4)
-    mixed = swap(mixed, "lat").transpose(2, 0, 1, 3, 4)
-    mixed = mixed.reshape(per_dev, order_total, 2 * block_ch)
-    back = jnp.einsum("mlj,mlc->mjc", legendre, mixed, preferred_element_type=jnp.float32)
-    back = (back * weights[None, :, None]).astype(jnp.bfloat16)
-    back = back.reshape(per_dev, lat_count, lat_rows, 2, block_ch).transpose(1, 2, 0, 3, 4)
-    back = swap(back, "lat").transpose(1, 0, 2, 3, 4).reshape(lat_rows, 2 * order_total, block_ch)
-    back = lax.all_gather(back, "lon", axis=0)
-    back = back.transpose(1, 2, 0, 3).reshape(lat_rows, 2 * order_total, channels)
-    grid_back = jnp.einsum("jqc,kq->jkc", back, forward, preferred_element_type=jnp.float32)
-    grid_back = grid_back.astype(jnp.bfloat16).astype(jnp.float32)
-    input_grad = (cotangent.astype(jnp.float32) + grid_back).astype(jnp.bfloat16)
-    coefficients = analyse(partial_spectrum(grid_input, forward, own_weights, lon_count))
-    weight_grad = jnp.einsum(
-        "lqi,lqc->lic", coefficients, full_adjoint, preferred_element_type=jnp.float32
-    )
+    scale = weights[:, None]
+    by_lat = (lat_count, -1, block_ch)
+    flat = (-1, block_ch)
+
+    part_g = partial_spectrum(
+        cotangent, backward.T, jnp.ones_like(own_weights), lat_count, lon_count
+    )
+    (part_g,) = exchange(0, ("lon", part_g))
+    part_x = partial_spectrum(grid_input, forward.T, own_weights, lat_count, lon_count)
+    part_x, rows_g = exchange(1, ("lon", part_x), ("lat", add_parts(part_g)))
+    adjoint = transform(True, legendre, scale, rows_g.reshape(flat))
+    (adjoint,) = exchange(2, ("spread", adjoint.reshape(by_lat)))
+    mixed = mix(adjoint, mixing)
+    mixed, rows_x = exchange(3, ("lat", mixed), ("lat", add_parts(part_x)))
+    back = transform(False, legendre, scale, mixed.reshape(flat))
+    coefficients = transform(True, legendre, scale, rows_x.reshape(flat))
+    back, coefficients = exchange(
+        4, ("spread", back.reshape(by_lat)), ("lat", coefficients.reshape(by_lat))
+    )
+    input_grad = grid_gradient(forward, back, cotangent)
+    weight_grad = weight_gradient(adjoint, coefficients, per_dev)
     return (input_grad, weight_grad)
 
 

time: 518 us -> 402 us (0.78); the launches traced: 507 us -> 401 us
  Pallas kernels: 5.29 us -> 373 us
  waiting for transfers between devices: 221 us -> 0 us
  blocking collectives: 85 us -> 0 us
  local copies, waits for them, and re-layouts: 84.7 us -> 15.4 us
  matrix products: 45.6 us -> 0 us
  starting transfers between devices: 38.1 us -> 0 us
  between operations: 14.7 us -> 0.92 us
    pallas_call x0 -> x13, Pallas kernels: none -> 368 us  [the longest x5 328 us: exchange(): pl.pallas_call(functools.partial(exchange_kernel, kinds, counts), out_sha...]
    all_to_all x6 -> x0, waiting for transfers between devices: 185 us -> none  [swap(): return lax.all_to_all(block, axis, split_axis=0, concat_axis=0, tiled=True)]
    all_to_all x2 -> x0, blocking collectives: 85 us -> none  [swap(): return lax.all_to_all(block, axis, split_axis=0, concat_axis=0, tiled=True)]
    reshape x14 -> x0, local copies, waits for them, and re-layouts: 49.6 us -> none  [the longest x2 11.8 us: analyse(): rows.transpose(1, 0, 3, 2, 4).reshape(per_dev, count_lat, 2 * block_ch)]
    dot_general x8 -> x0, matrix products: 45.6 us -> none  [the longest x2 18.9 us: partial_spectrum(): jnp.einsum('jkc,kq->jqc', field, table, preferred_element_type=jnp.float32)]
    all_to_all x6 -> x0, starting transfers between devices: 37.8 us -> none  [swap(): return lax.all_to_all(block, axis, split_axis=0, concat_axis=0, tiled=True)]
    all_gather x2 -> x0, waiting for transfers between devices: 35.9 us -> none  [the longest x1 35.9 us: local(): full_adjoint = lax.all_gather(adjoint, 'lon', axis=0)]
    transpose x6 -> x1, local copies, waits for them, and re-layouts: 21.2 us -> 0.25 us  [local(): part_x = partial_spectrum(grid_input, forward.T, own_weights, lat_count,...]
  transfers between devices with their start and end apart: 8 -> 0, of which waited for: 7 -> 0; matrix products, arithmetic and copies ran while one was open for 16% -> 0% of each run, Pallas kernels for 1% -> 0%
where the time goes in v2:
time: 402 us; the launch traced here: 401 us
  Pallas kernels  373 us (93%)
  local copies, waits for them, and re-layouts  15.4 us (4%)
  other arithmetic  11.9 us (3%)
    pallas_call x5, Pallas kernels, exchange(): pl.pallas_call(functools.partial(exchange_kernel, kinds, counts), out_sha...  328 us
    pallas_call x2, Pallas kernels, partial_spectrum(): pl.pallas_call(functools.partial(spectrum_kernel, lon_count), grid=(rows...  19.9 us
    unnamed x22, local copies, waits for them, and re-layouts  12.9 us
    pallas_call x1, Pallas kernels, grid_gradient(): pl.pallas_call(grid_kernel, grid=(rows // PAIR,), out_shape=jax.ShapeDtyp...  12.4 us
    reduce_sum x2, other arithmetic, add_parts(): return jnp.sum(parts.astype(jnp.float32), axis=0).astype(jnp.bfloat16)  8.14 us

profile of v2, /device:TPU:27, one launch (start us, length us, event | category | flops | bytes accessed | tf_op | source)
XLA Modules:
  0.0 401.5 jit_solution(17328134009582447191)
XLA Ops:
  0.8 2.5 fusion.5
  3.3 0.9 copy.11
  4.2 0.8 reshape.178
  5.1 0.3 copy.12.table_ref
  5.3 0.3 copy.13.table_ref
  5.6 10.0 %shard_map.51.refs_0_ = bf16[2,16,528,128]{3,2,1,0:T(8,128)(2,1)S(1)} custom-call(f32[22]{0:T(128)S(1)} %dynamic_slice.3.scale_ref, bf16[384,720]{1,0:T(8,128)(2,1)S(1)} %copy.13.table_ref, bf16[22,720,256]{2,1,0:T(8,128)(2,1)} %field_ref.3), custom_call_target="tpu_custom_call" | custom-call | tf_op jit(solution)/shard_map/pallas_call | solution.py:253
  15.7 2.0 copy-done.2
  18.1 9.9 %shard_map.52.refs_0_ = bf16[2,16,528,128]{3,2,1,0:T(8,128)(2,1)S(1)} custom-call(f32[22]{0:T(128)S(1)} %broadcast_7_scale_ref.2.scale_ref, bf16[384,720]{1,0:T(8,128)(2,1)S(1)} %fusion.2.table_ref, bf16[22,720,256]{2,1,0:T(8,128)(2,1)} %field_ref.5), custom_call_target="tpu_custom_call" | custom-call | tf_op jit(solution)/shard_map/pallas_call | solution.py:253
  28.0 2.0 copy-done.3
  30.0 48.2 %shard_map.53 = bf16[2,16,528,128]{3,2,1,0:T(8,128)(2,1)S(1)} custom-call(bf16[2,16,528,128]{3,2,1,0:T(8,128)(2,1)} %copy-done.3), custom_call_target="tpu_custom_call" | custom-call | tf_op jit(solution)/shard_map/pallas_call | solution.py:220
  78.2 2.0 copy-done.4
  80.2 3.2 reduce_sum.34.refs_1_
  83.3 68.9 %shard_map.54 = (bf16[2,16,528,128]{3,2,1,0:T(8,128)(2,1)}, bf16[16,528,128]{2,1,0:T(8,128)(2,1)S(1)}) custom-call(bf16[2,16,528,128]{3,2,1,0:T(8,128)(2,1)} %copy-done.2, bf16[16,528,128]{2,1,0:T(8,128)(2,1)S(1)} %reduce_sum.34.refs_1_), custom_call_target="tpu_custom_call" | custom-call | tf_op jit(solution)/shard_map/pallas_call | solution.py:220
  152.2 1.3 copy-done.8
  153.6 0.2 select_reduce_fusion
  154.0 5.3 %shard_map.50.legendre_ref = bf16[12,192,352]{2,1,0:T(8,128)(2,1)S(1)} custom-call(f32[12,1]{1,0:T(8,128)S(1)} %add_convert_fusion.order_ref, f32[1,352]{1,0:T(1,128)S(1)} %multiply_cosine_fusion.cosine_ref, f32[12,352]{1,0:T(8,128)S(1)} %multiply_add_fusion.start_ref), custom_call_target="tpu_custom_call" | custom-call | tf_op jit(solution)/shard_map/pallas_call | solution.py:72
  159.3 0.6 sine_multiply_fusion.scale_ref
  160.0 1.6 copy-done.9
  161.6 1.6 shard_map.55
  163.1 46.3 %shard_map.56.adjoint_ref = bf16[2,16,288,128]{3,2,1,0:T(8,128)(2,1)S(1)} custom-call(bf16[16,288,128]{2,1,0:T(8,128)(2,1)S(1)} %bitcast.14), custom_call_target="tpu_custom_call" | custom-call | tf_op jit(solution)/shard_map/pallas_call | solution.py:220
  209.5 0.8 shard_map.57.refs_0_
  210.2 0.6 copy-done
  210.9 1.0 copy-done.5
  211.9 5.0 %reduce_sum.35.refs_1_ = bf16[16,528,128]{2,1,0:T(8,128)(2,1)} reduce(bf16[2,16,528,128]{3,2,1,0:T(8,128)(2,1)} %get-tuple-element.9, bf16[]{:T(256)} %constant.53.clone.1), dimensions={0}, to_apply=%region_2.3 | reduce | flops 1081344 | bytes 6488066 | tf_op jit(solution)/shard_map/reduce_sum | solution.py:410
  216.9 1.3 copy-done.6
  218.1 77.2 %shard_map.58 = (bf16[16,288,128]{2,1,0:T(8,128)(2,1)S(1)}, bf16[16,528,128]{2,1,0:T(8,128)(2,1)S(1)}) custom-call(bf16[16,288,128]{2,1,0:T(8,128)(2,1)S(1)} %copy-done.6, bf16[16,528,128]{2,1,0:T(8,128)(2,1)} %reduce_sum.35.refs_1_), custom_call_target="tpu_custom_call" | custom-call | tf_op jit(solution)/shard_map/pallas_call | solution.py:220
  295.4 1.6 shard_map.60
  296.9 1.8 shard_map.59
  298.8 87.4 %shard_map.61 = (bf16[2,16,528,128]{3,2,1,0:T(8,128)(2,1)}, bf16[16,288,128]{2,1,0:T(8,128)(2,1)S(1)}) custom-call(bf16[16,528,128]{2,1,0:T(8,128)(2,1)S(1)} %bitcast.11, bf16[16,288,128]{2,1,0:T(8,128)(2,1)S(1)} %bitcast.13), custom_call_target="tpu_custom_call" | custom-call | tf_op jit(solution)/shard_map/pallas_call | solution.py:220
  386.3 1.8 shard_map.63
  388.1 1.0 copy-done.7
  389.1 12.4 %shard_map.62 = bf16[22,720,256]{2,1,0:T(8,128)(2,1)} custom-call(bf16[720,384]{1,0:T(8,128)(2,1)S(1)} %copy.12.table_ref, bf16[2,16,528,128]{3,2,1,0:T(8,128)(2,1)S(1)} %copy-done.7, bf16[22,720,256]{2,1,0:T(8,128)(2,1)} %field_ref.5), custom_call_target="tpu_custom_call" | custom-call | tf_op jit(solution)/shard_map/pallas_call | solution.py:393
  (29 shorter events, 0.8 us)
Async XLA Ops:
  15.6 2.1 copy-start.2
  28.0 2.0 copy-start.3
  78.2 2.0 copy-start.4
  152.2 1.3 copy-start.8
  160.0 1.6 copy-start.9
  163.1 46.3 %copy-start.10 = (bf16[12,128,256]{2,1,0:T(8,128)(2,1)S(1)}, bf16[12,128,256]{2,1,0:T(8,128)(2,1)}, u32[]{:S(2)}) copy-start(bf16[12,128,256]{2,1,0:T(8,128)(2,1)} %mixing_ref.1) | copy-start | bytes 2359300
  209.5 1.4 copy-start
  210.9 1.0 copy-start.5
  216.9 1.3 copy-start.6
  298.8 87.5 %copy-start.1 = (bf16[2,16,288,128]{3,2,1,0:T(8,128)(2,1)S(1)}, bf16[2,16,288,128]{3,2,1,0:T(8,128)(2,1)}, u32[]{:S(2)}) copy-start(bf16[2,16,288,128]{3,2,1,0:T(8,128)(2,1)} %copy-done) | copy-start | bytes 7077892
  386.3 2.8 copy-start.7

commit v3 on v2

--- a/solution.py
+++ b/solution.py
@@ -105,39 +105,149 @@
     return lax.rem(lax.axis_index(axis) + offset + count, count)
 
 
-def swap_copy(source, target, sems, axis, count, offset):
-    there = peer(axis, count, offset)
-    return pltpu.make_async_remote_copy(
-        src_ref=source.at[there],
-        dst_ref=target.at[lax.axis_index(axis)],
-        send_sem=sems.at[0, offset],
-        recv_sem=sems.at[1, offset],
-        device_id={axis: there},
-        device_id_type=MESH,
-    )
-
-
-def spread_copy(target, slot, sems, offset, step, lon_count):
-    here = lax.axis_index("lon")
-    return pltpu.make_async_remote_copy(
-        src_ref=target.at[here, slot],
-        dst_ref=target.at[here, slot],
-        send_sem=sems.at[0, offset, step],
-        recv_sem=sems.at[1, offset, step],
-        device_id={"lon": peer("lon", lon_count, offset)},
-        device_id_type=MESH,
-    )
-
-
-def exchange_kernel(jobs, counts, *refs):
-    total = len(jobs)
-    sources, targets, sems = refs[:total], refs[total : 2 * total], refs[2 * total :]
-    lat_count, lon_count = counts["lat"], counts["lon"]
-    axes = [axis for axis in ("lon", "lat") if axis in jobs or "spread" in jobs]
+class Swap:
+    def __init__(self, counts, source, target, landing, own_sem, sems):
+        self.counts, self.source, self.target = counts, source, target
+        self.landing, self.sems = landing, sems
+        self.here = lax.axis_index("lat")
+        self.own = pltpu.make_async_copy(
+            source.at[self.here], landing.at[self.here], own_sem
+        )
+
+    def copy(self, offset):
+        there = peer("lat", self.counts["lat"], offset)
+        return pltpu.make_async_remote_copy(
+            src_ref=self.source.at[there],
+            dst_ref=self.landing.at[self.here],
+            send_sem=self.sems.at[0, offset],
+            recv_sem=self.sems.at[1, offset],
+            device_id={"lat": there},
+            device_id_type=MESH,
+        )
+
+    def each(self, act):
+        def body(offset, carried):
+            act(self.copy(offset))
+            return carried
+
+        lax.fori_loop(1, self.counts["lat"], body, 0)
+
+    def start(self):
+        self.each(lambda copy: copy.start())
+        self.own.start()
+
+    def first(self):
+        pass
+
+    def step(self, offset):
+        pass
+
+    def finish(self):
+        self.own.wait()
+        self.each(lambda copy: copy.wait())
+
+
+class Spread(Swap):
+    def __init__(self, counts, source, target, own_sem, sems, further):
+        super().__init__(
+            counts, source, target, target.at[lax.axis_index("lon")], own_sem, sems
+        )
+        self.further = further
+
+    def onward(self, offset, ahead):
+        slot = peer("lat", self.counts["lat"], -offset)
+        return pltpu.make_async_remote_copy(
+            src_ref=self.landing.at[slot],
+            dst_ref=self.landing.at[slot],
+            send_sem=self.further.at[0, ahead, offset],
+            recv_sem=self.further.at[1, ahead, offset],
+            device_id={"lon": peer("lon", self.counts["lon"], ahead)},
+            device_id_type=MESH,
+        )
+
+    def first(self):
+        self.own.wait()
+        for ahead in range(1, self.counts["lon"]):
+            self.onward(0, ahead).start()
+
+    def step(self, offset):
+        self.copy(offset).wait_recv()
+        for ahead in range(1, self.counts["lon"]):
+            self.onward(offset, ahead).start()
+
+    def finish(self):
+        self.each(lambda copy: copy.wait_send())
+
+        def body(offset, carried):
+            for ahead in range(1, self.counts["lon"]):
+                self.onward(offset, ahead).wait()
+            return carried
+
+        lax.fori_loop(0, self.counts["lat"], body, 0)
+
+
+class Reduce(Swap):
+    def __init__(self, counts, source, target, own_sem, sems, further, sums, arrived, load_sem):
+        super().__init__(counts, sums, target, target, own_sem, sems)
+        self.parts, self.further, self.sums, self.arrived = source, further, sums, arrived
+        self.load = pltpu.make_async_copy(source.at[lax.axis_index("lon")], sums, load_sem)
+
+    def across(self, offset, ahead):
+        slot = peer("lat", self.counts["lat"], offset)
+        there = peer("lon", self.counts["lon"], ahead)
+        return pltpu.make_async_remote_copy(
+            src_ref=self.parts.at[there, slot],
+            dst_ref=self.arrived.at[ahead - 1, slot],
+            send_sem=self.further.at[0, ahead, offset],
+            recv_sem=self.further.at[1, ahead, offset],
+            device_id={"lon": there},
+            device_id_type=MESH,
+        )
+
+    def every(self, begin, act):
+        def body(offset, carried):
+            for ahead in range(1, self.counts["lon"]):
+                act(self.across(offset, ahead))
+            return carried
+
+        lax.fori_loop(begin, self.counts["lat"], body, 0)
+
+    def start(self):
+        self.load.start()
+        self.every(1, lambda copy: copy.start())
+        for ahead in range(1, self.counts["lon"]):
+            self.across(0, ahead).start()
+
+    def first(self):
+        self.load.wait()
+
+    def add(self, offset):
+        slot = peer("lat", self.counts["lat"], offset)
+        total = self.sums[slot].astype(jnp.float32)
+        for ahead in range(1, self.counts["lon"]):
+            self.across(offset, ahead).wait_recv()
+            total = total + self.arrived[ahead - 1, slot].astype(jnp.float32)
+        self.sums[slot] = total.astype(jnp.bfloat16)
+
+    def step(self, offset):
+        self.add(offset)
+        self.copy(offset).start()
+
+    def finish(self):
+        self.add(0)
+        self.own.start()
+        self.own.wait()
+        self.each(lambda copy: copy.wait())
+        self.every(0, lambda copy: copy.wait_send())
+
+
+def exchange_kernel(kinds, counts, lengths, *refs):
+    total = len(kinds)
+    sources, targets, scratch = refs[:total], refs[total : 2 * total], refs[2 * total :]
 
     barrier = pltpu.get_barrier_semaphore()
     expected = 0
-    for axis in axes:
+    for axis in ("lon", "lat") if set(kinds) != {Swap} else ("lat",):
 
         def greet(offset, carried, axis=axis):
             there = peer(axis, counts[axis], offset)
@@ -148,77 +258,52 @@
         expected += counts[axis] - 1
     pl.semaphore_wait(barrier, expected)
 
-    place = 0
-    plans = []
-    for kind, source, target in zip(jobs, sources, targets):
-        axis = "lat" if kind == "spread" else kind
-        landing = target.at[lax.axis_index("lon")] if kind == "spread" else target
-        own = pltpu.make_async_copy(
-            source.at[lax.axis_index(axis)], landing.at[lax.axis_index(axis)], sems[place]
-        )
-        plans.append((kind, axis, source, landing, target, own, sems[place + 1], sems[place + 2]))
-        place += 3
-    for kind, axis, source, landing, target, own, first, second in plans:
-
-        def start(offset, carried, plan=(source, landing, first, axis, counts[axis])):
-            swap_copy(*plan, offset).start()
+    jobs, place = [], 0
+    for kind, length, source, target in zip(kinds, lengths, sources, targets):
+        held = scratch[place : place + length]
+        landing = (target,) if kind is Swap else ()
+        jobs.append(kind(counts, source, target, *landing, *held))
+        place += length
+    for job in jobs:
+        job.start()
+    for job in jobs:
+        job.first()
+
+    if set(kinds) != {Swap}:
+
+        def body(offset, carried):
+            for job in jobs:
+                job.step(offset)
             return carried
 
-        lax.fori_loop(1, counts[axis], start, 0)
-        own.start()
-    for kind, axis, source, landing, target, own, first, second in plans:
-        own.wait()
-        if kind == "spread":
-            for ahead in range(1, lon_count):
-                spread_copy(target, peer("lat", lat_count, 0), second, ahead, 0, lon_count).start()
-
-        def arrive(offset, carried, plan=(source, landing, first, axis, counts[axis])):
-            swap_copy(*plan, offset).wait_recv()
-            return carried
-
-        def arrive_and_spread(offset, carried, target=target, second=second, arrive=arrive):
-            arrive(offset, carried)
-            slot = peer("lat", lat_count, -offset)
-            for ahead in range(1, lon_count):
-                spread_copy(target, slot, second, ahead, offset, lon_count).start()
-            return carried
-
-        lax.fori_loop(1, counts[axis], arrive_and_spread if kind == "spread" else arrive, 0)
-    for kind, axis, source, landing, target, own, first, second in plans:
-
-        def leave(offset, carried, plan=(source, landing, first, axis, counts[axis])):
-            swap_copy(*plan, offset).wait_send()
-            return carried
-
-        lax.fori_loop(1, counts[axis], leave, 0)
-        if kind == "spread":
-
-            def finish(offset, carried, target=target, second=second):
-                slot = peer("lat", lat_count, -offset)
-                for ahead in range(1, lon_count):
-                    copy = spread_copy(target, slot, second, ahead, offset, lon_count)
-                    copy.wait_send()
-                    copy.wait_recv()
-                return carried
-
-            lax.fori_loop(0, lat_count, finish, 0)
+        lax.fori_loop(1, counts["lat"], body, 0)
+    for job in jobs:
+        job.finish()
 
 
 def exchange(ident, *pairs):
     counts = {"lat": lax.axis_size("lat"), "lon": lax.axis_size("lon")}
     kinds = [kind for kind, _ in pairs]
     arrays = [array for _, array in pairs]
-    shapes, scratch = [], []
+    dma = pltpu.SemaphoreType.DMA
+    shapes, scratch, lengths = [], [], []
     for kind, array in pairs:
-        shape = (counts["lon"],) + array.shape if kind == "spread" else array.shape
+        shape = array.shape
+        held = [dma, dma((2, counts["lat"]))]
+        if kind is not Swap:
+            held.append(dma((2, counts["lon"], counts["lat"])))
+        if kind is Spread:
+            shape = (counts["lon"],) + shape
+        if kind is Reduce:
+            shape = shape[1:]
+            held.append(pltpu.VMEM(shape, array.dtype))
+            held.append(pltpu.VMEM((counts["lon"] - 1,) + shape, array.dtype))
+            held.append(dma)
         shapes.append(jax.ShapeDtypeStruct(shape, array.dtype))
-        axis = "lat" if kind == "spread" else kind
-        scratch.append(pltpu.SemaphoreType.DMA)
-        scratch.append(pltpu.SemaphoreType.DMA((2, counts[axis])))
-        further = (2, counts["lon"], counts["lat"]) if kind == "spread" else (1,)
-        scratch.append(pltpu.SemaphoreType.DMA(further))
-    return pl.pallas_call(
-        functools.partial(exchange_kernel, kinds, counts),
+        scratch += held
+        lengths.append(len(held))
+    return pl.pallas_call(
+        functools.partial(exchange_kernel, kinds, counts, lengths),
         out_shape=shapes,
         in_specs=[ANY] * len(arrays),
         out_specs=[ANY] * len(arrays),
@@ -404,10 +489,6 @@
         out_specs=pl.BlockSpec(block, lambda i: (i, 0, 0)),
         compiler_params=limits(),
     )(table, back, field)
-
-
-def add_parts(parts):
-    return jnp.sum(parts.astype(jnp.float32), axis=0).astype(jnp.bfloat16)
 
 
 def local(grid_input, cotangent, mixing):
@@ -434,17 +515,15 @@
     part_g = partial_spectrum(
         cotangent, backward.T, jnp.ones_like(own_weights), lat_count, lon_count
     )
-    (part_g,) = exchange(0, ("lon", part_g))
+    (rows_g,) = exchange(0, (Reduce, part_g))
     part_x = partial_spectrum(grid_input, forward.T, own_weights, lat_count, lon_count)
-    part_x, rows_g = exchange(1, ("lon", part_x), ("lat", add_parts(part_g)))
     adjoint = transform(True, legendre, scale, rows_g.reshape(flat))
-    (adjoint,) = exchange(2, ("spread", adjoint.reshape(by_lat)))
-    mixed = mix(adjoint, mixing)
-    mixed, rows_x = exchange(3, ("lat", mixed), ("lat", add_parts(part_x)))
+    adjoint, rows_x = exchange(1, (Spread, adjoint.reshape(by_lat)), (Reduce, part_x))
+    (mixed,) = exchange(2, (Swap, mix(adjoint, mixing)))
     back = transform(False, legendre, scale, mixed.reshape(flat))
     coefficients = transform(True, legendre, scale, rows_x.reshape(flat))
     back, coefficients = exchange(
-        4, ("spread", back.reshape(by_lat)), ("lat", coefficients.reshape(by_lat))
+        3, (Spread, back.reshape(by_lat)), (Swap, coefficients.reshape(by_lat))
     )
     input_grad = grid_gradient(forward, back, cotangent)
     weight_grad = weight_gradient(adjoint, coefficients, per_dev)

time: 402 us -> 322 us (0.80)
  Pallas kernels: 373 us -> 305 us
  other arithmetic: 11.9 us -> 3.77 us
  local copies, waits for them, and re-layouts: 15.4 us -> 11.1 us
    pallas_call x5 -> x4, Pallas kernels: 328 us -> 260 us  [exchange(): pl.pallas_call(functools.partial(exchange_kernel, kinds, counts, lengths)...]
    reduce_sum x2 -> x0, other arithmetic: 8.14 us -> none  [add_parts(): return jnp.sum(parts.astype(jnp.float32), axis=0).astype(jnp.bfloat16)]
    unnamed x22 -> x8, local copies, waits for them, and re-layouts: 12.9 us -> 6.26 us
where the time goes in v3:
time: 322 us; the launch traced here: 321 us
  Pallas kernels  305 us (95%)
  local copies, waits for them, and re-layouts  11.1 us (3%)
  other arithmetic  3.77 us (1%)
    pallas_call x4, Pallas kernels, exchange(): pl.pallas_call(functools.partial(exchange_kernel, kinds, counts, lengths)...  260 us
    pallas_call x2, Pallas kernels, partial_spectrum(): pl.pallas_call(functools.partial(spectrum_kernel, lon_count), grid=(rows...  19.7 us
    pallas_call x1, Pallas kernels, grid_gradient(): pl.pallas_call(grid_kernel, grid=(rows // PAIR,), out_shape=jax.ShapeDtyp...  12.4 us

profile of v3, /device:TPU:27, one launch (start us, length us, event | category | flops | bytes accessed | tf_op | source)
XLA Modules:
  0.0 320.8 jit_solution(3452810149590171361)
XLA Ops:
  0.7 0.1 multiply_cosine_fusion.cosine_ref
  0.8 0.1 dynamic_slice.3.scale_ref
  0.9 0.2 select_reduce_fusion
  1.2 0.1 multiply_add_fusion.start_ref
  1.2 0.1 broadcast_in_dim.32
  1.3 0.1 mul.143
  1.5 0.6 sine_multiply_fusion.scale_ref
  2.1 2.5 fusion.5
  4.6 0.1 pad_maximum_fusion
  4.7 1.9 copy.11
  6.6 2.1 reshape.178
  8.7 0.3 copy.12.table_ref
  9.0 0.1 fusion.2.table_ref
  9.1 0.3 copy.13.table_ref
  9.4 5.3 %shard_map.50.legendre_ref = bf16[12,192,352]{2,1,0:T(8,128)(2,1)S(1)} custom-call(f32[12,1]{1,0:T(8,128)S(1)} %add_convert_fusion.order_ref, f32[1,352]{1,0:T(1,128)S(1)} %multiply_cosine_fusion.cosine_ref, f32[12,352]{1,0:T(8,128)S(1)} %multiply_add_fusion.start_ref), custom_call_target="tpu_custom_call" | custom-call | tf_op jit(solution)/shard_map/pallas_call | solution.py:72
  14.7 9.9 %shard_map.54.refs_1_ = bf16[2,16,528,128]{3,2,1,0:T(8,128)(2,1)S(1)} custom-call(f32[22]{0:T(128)S(1)} %dynamic_slice.3.scale_ref, bf16[384,720]{1,0:T(8,128)(2,1)S(1)} %copy.13.table_ref, bf16[22,720,256]{2,1,0:T(8,128)(2,1)} %field_ref.4), custom_call_target="tpu_custom_call" | custom-call | tf_op jit(solution)/shard_map/pallas_call | solution.py:338
  24.5 2.0 copy-done.1
  26.5 9.9 %shard_map.51.refs_0_ = bf16[2,16,528,128]{3,2,1,0:T(8,128)(2,1)S(1)} custom-call(f32[22]{0:T(128)S(1)} %broadcast_7_scale_ref.2.scale_ref, bf16[384,720]{1,0:T(8,128)(2,1)S(1)} %fusion.2.table_ref, bf16[22,720,256]{2,1,0:T(8,128)(2,1)} %field_ref.5), custom_call_target="tpu_custom_call" | custom-call | tf_op jit(solution)/shard_map/pallas_call | solution.py:338
  36.4 0.0 copy-start
  36.4 2.0 copy-done
  38.4 64.6 %shard_map.52 = bf16[16,528,128]{2,1,0:T(8,128)(2,1)S(1)} custom-call(bf16[2,16,528,128]{3,2,1,0:T(8,128)(2,1)} %copy-done), custom_call_target="tpu_custom_call" | custom-call | tf_op jit(solution)/shard_map/pallas_call | solution.py:305
  103.0 1.5 shard_map.53
  104.6 77.9 %shard_map.55 = (bf16[2,16,288,128]{3,2,1,0:T(8,128)(2,1)S(1)}, bf16[16,528,128]{2,1,0:T(8,128)(2,1)S(1)}) custom-call(bf16[16,288,128]{2,1,0:T(8,128)(2,1)S(1)} %bitcast.16, bf16[2,16,528,128]{3,2,1,0:T(8,128)(2,1)} %copy-done.1), custom_call_target="tpu_custom_call" | custom-call | tf_op jit(solution)/shard_map/pallas_call | solution.py:305
  182.5 0.0 copy-start.3
  182.5 1.5 shard_map.59
  184.1 0.8 shard_map.56.refs_0_
  184.9 30.0 %shard_map.57 = bf16[16,288,128]{2,1,0:T(8,128)(2,1)S(1)} custom-call(bf16[16,288,128]{2,1,0:T(8,128)(2,1)S(1)} %shard_map.56.refs_0_), custom_call_target="tpu_custom_call" | custom-call | tf_op jit(solution)/shard_map/pallas_call | solution.py:305
  214.9 1.8 shard_map.58
  216.7 87.8 %shard_map.60 = (bf16[2,16,528,128]{3,2,1,0:T(8,128)(2,1)}, bf16[16,288,128]{2,1,0:T(8,128)(2,1)S(1)}) custom-call(bf16[16,528,128]{2,1,0:T(8,128)(2,1)S(1)} %bitcast.11, bf16[16,288,128]{2,1,0:T(8,128)(2,1)S(1)} %bitcast.14), custom_call_target="tpu_custom_call" | custom-call | tf_op jit(solution)/shard_map/pallas_call | solution.py:305
  304.4 1.8 shard_map.62
  306.2 2.2 copy-done.2
  308.5 12.4 %shard_map.61 = bf16[22,720,256]{2,1,0:T(8,128)(2,1)} custom-call(bf16[720,384]{1,0:T(8,128)(2,1)S(1)} %copy.12.table_ref, bf16[2,16,528,128]{3,2,1,0:T(8,128)(2,1)S(1)} %copy-done.2, bf16[22,720,256]{2,1,0:T(8,128)(2,1)} %field_ref.5), custom_call_target="tpu_custom_call" | custom-call | tf_op jit(solution)/shard_map/pallas_call | solution.py:478
  (12 shorter events, 0.1 us)
Async XLA Ops:
  24.5 2.0 copy-start.1
  36.4 2.1 copy-start
  182.5 1.6 copy-start.3
  306.2 2.2 copy-start.2

commit v4 on v3

--- a/solution.py
+++ b/solution.py
@@ -80,15 +80,18 @@
 
 
 def fourier_tables(order_ids, first, points_held, count_lon):
+    def angles(order, part, point):
+        index = 4 * (point * order) + part * count_lon
+        return (index % (4 * count_lon)).astype(jnp.float32) * (0.5 * math.pi / count_lon)
+
     points = first + jnp.arange(points_held, dtype=jnp.int32)
-    phase_index = points[:, None] * order_ids[None, :] % count_lon
-    angles = phase_index.astype(jnp.float32) * (2.0 * math.pi / count_lon)
-    forward = jnp.stack([jnp.cos(angles), -jnp.sin(angles)], axis=2).reshape(
-        points_held, 2 * order_ids.shape[0]
-    )
-    factor = jnp.where(order_ids == 0, 1.0, 2.0).astype(jnp.float32) / count_lon
-    backward = forward * jnp.repeat(factor, 2)[None, :]
-    return (forward.astype(jnp.bfloat16), backward.astype(jnp.bfloat16))
+    slots = jnp.repeat(order_ids, 2)
+    parts = jnp.arange(slots.shape[0], dtype=jnp.int32) % 2
+    forward = jnp.cos(angles(slots[None, :], parts[None, :], points[:, None]))
+    forward_rows = jnp.cos(angles(slots[:, None], parts[:, None], points[None, :]))
+    factor = jnp.where(slots == 0, 1.0, 2.0).astype(jnp.float32) / count_lon
+    tables = (forward, forward_rows, forward_rows * factor[:, None])
+    return tuple(table.astype(jnp.bfloat16) for table in tables)
 
 
 MESH = pl.DeviceIdType.MESH
@@ -106,89 +109,134 @@
 
 
 class Swap:
-    def __init__(self, counts, source, target, landing, own_sem, sems):
-        self.counts, self.source, self.target = counts, source, target
+    def __init__(self, counts, reach, source, target, landing, own_sem, sems):
+        self.counts, self.reach, self.source, self.target = counts, reach, source, target
         self.landing, self.sems = landing, sems
         self.here = lax.axis_index("lat")
+        self.chunks = sems.shape[2]
         self.own = pltpu.make_async_copy(
             source.at[self.here], landing.at[self.here], own_sem
         )
 
-    def copy(self, offset):
+    def rows(self, chunk):
+        height = self.landing.shape[1] // self.chunks
+        return pl.ds(chunk * height, height)
+
+    def copy(self, offset, chunk):
         there = peer("lat", self.counts["lat"], offset)
         return pltpu.make_async_remote_copy(
-            src_ref=self.source.at[there],
-            dst_ref=self.landing.at[self.here],
-            send_sem=self.sems.at[0, offset],
-            recv_sem=self.sems.at[1, offset],
+            src_ref=self.source.at[there, self.rows(chunk)],
+            dst_ref=self.landing.at[self.here, self.rows(chunk)],
+            send_sem=self.sems.at[0, offset, chunk],
+            recv_sem=self.sems.at[1, offset, chunk],
             device_id={"lat": there},
             device_id_type=MESH,
         )
 
+    def each_chunk(self, sender, receiver, act):
+        if self.reach is None:
+            act(0)
+            return
+        orders, degrees = (sender, receiver) if self.reach == "out" else (receiver, sender)
+        per_dev = self.counts["orders"]
+        for chunk in range(self.chunks):
+            least = orders + self.counts["lat"] * (per_dev // self.chunks) * chunk
+            pl.when(least < (degrees + 1) * per_dev)(functools.partial(act, chunk))
+
+    def send(self, offset):
+        there = peer("lat", self.counts["lat"], offset)
+        self.each_chunk(self.here, there, lambda chunk: self.copy(offset, chunk).start())
+
+    def sent(self, offset):
+        there = peer("lat", self.counts["lat"], offset)
+        self.each_chunk(self.here, there, lambda chunk: self.copy(offset, chunk).wait_send())
+
+    def receive(self, offset, then=None):
+        origin = peer("lat", self.counts["lat"], -offset)
+
+        def act(chunk):
+            self.copy(offset, chunk).wait_recv()
+            if then is not None:
+                then(chunk)
+
+        self.each_chunk(origin, self.here, act)
+
     def each(self, act):
         def body(offset, carried):
-            act(self.copy(offset))
+            act(offset)
             return carried
 
         lax.fori_loop(1, self.counts["lat"], body, 0)
 
-    def start(self):
-        self.each(lambda copy: copy.start())
+    def start(self, alone):
         self.own.start()
+        if alone:
+            self.each(self.send)
 
     def first(self):
         pass
 
     def step(self, offset):
-        pass
+        self.send(offset)
 
     def finish(self):
         self.own.wait()
-        self.each(lambda copy: copy.wait())
+        self.each(self.receive)
+        self.each(self.sent)
 
 
 class Spread(Swap):
-    def __init__(self, counts, source, target, own_sem, sems, further):
+    def __init__(self, counts, reach, source, target, own_sem, sems, further):
         super().__init__(
-            counts, source, target, target.at[lax.axis_index("lon")], own_sem, sems
+            counts, reach, source, target, target.at[lax.axis_index("lon")], own_sem, sems
         )
         self.further = further
 
-    def onward(self, offset, ahead):
+    def onward(self, offset, chunk, ahead):
         slot = peer("lat", self.counts["lat"], -offset)
         return pltpu.make_async_remote_copy(
-            src_ref=self.landing.at[slot],
-            dst_ref=self.landing.at[slot],
-            send_sem=self.further.at[0, ahead, offset],
-            recv_sem=self.further.at[1, ahead, offset],
+            src_ref=self.landing.at[slot, self.rows(chunk)],
+            dst_ref=self.landing.at[slot, self.rows(chunk)],
+            send_sem=self.further.at[0, ahead, offset, chunk],
+            recv_sem=self.further.at[1, ahead, offset, chunk],
             device_id={"lon": peer("lon", self.counts["lon"], ahead)},
             device_id_type=MESH,
         )
 
+    def pass_on(self, offset, chunk):
+        for ahead in range(1, self.counts["lon"]):
+            self.onward(offset, chunk, ahead).start()
+
+    def start(self, alone):
+        self.own.start()
+        self.each(self.send)
+
     def first(self):
         self.own.wait()
-        for ahead in range(1, self.counts["lon"]):
-            self.onward(0, ahead).start()
+        self.each_chunk(self.here, self.here, lambda chunk: self.pass_on(0, chunk))
 
     def step(self, offset):
-        self.copy(offset).wait_recv()
-        for ahead in range(1, self.counts["lon"]):
-            self.onward(offset, ahead).start()
+        self.receive(offset, lambda chunk: self.pass_on(offset, chunk))
 
     def finish(self):
-        self.each(lambda copy: copy.wait_send())
+        self.each(self.sent)
 
         def body(offset, carried):
-            for ahead in range(1, self.counts["lon"]):
-                self.onward(offset, ahead).wait()
+            def act(chunk):
+                for ahead in range(1, self.counts["lon"]):
+                    self.onward(offset, chunk, ahead).wait()
+
+            self.each_chunk(peer("lat", self.counts["lat"], -offset), self.here, act)
             return carried
 
         lax.fori_loop(0, self.counts["lat"], body, 0)
 
 
 class Reduce(Swap):
-    def __init__(self, counts, source, target, own_sem, sems, further, sums, arrived, load_sem):
-        super().__init__(counts, sums, target, target, own_sem, sems)
+    def __init__(
+        self, counts, reach, source, target, own_sem, sems, further, sums, arrived, load_sem
+    ):
+        super().__init__(counts, None, sums, target, target, own_sem, sems)
         self.parts, self.further, self.sums, self.arrived = source, further, sums, arrived
         self.load = pltpu.make_async_copy(source.at[lax.axis_index("lon")], sums, load_sem)
 
@@ -212,7 +260,7 @@
 
         lax.fori_loop(begin, self.counts["lat"], body, 0)
 
-    def start(self):
+    def start(self, alone):
         self.load.start()
         self.every(1, lambda copy: copy.start())
         for ahead in range(1, self.counts["lon"]):
@@ -231,17 +279,18 @@
 
     def step(self, offset):
         self.add(offset)
-        self.copy(offset).start()
+        self.send(offset)
 
     def finish(self):
         self.add(0)
         self.own.start()
         self.own.wait()
-        self.each(lambda copy: copy.wait())
+        self.each(self.receive)
+        self.each(self.sent)
         self.every(0, lambda copy: copy.wait_send())
 
 
-def exchange_kernel(kinds, counts, lengths, *refs):
+def exchange_kernel(kinds, reaches, counts, lengths, *refs):
     total = len(kinds)
     sources, targets, scratch = refs[:total], refs[total : 2 * total], refs[2 * total :]
 
@@ -259,13 +308,13 @@
     pl.semaphore_wait(barrier, expected)
 
     jobs, place = [], 0
-    for kind, length, source, target in zip(kinds, lengths, sources, targets):
+    for kind, reach, length, source, target in zip(kinds, reaches, lengths, sources, targets):
         held = scratch[place : place + length]
         landing = (target,) if kind is Swap else ()
-        jobs.append(kind(counts, source, target, *landing, *held))
+        jobs.append(kind(counts, reach, source, target, *landing, *held))
         place += length
     for job in jobs:
-        job.start()
+        job.start(len(jobs) == 1)
     for job in jobs:
         job.first()
 
@@ -281,16 +330,22 @@
         job.finish()
 
 
-def exchange(ident, *pairs):
-    counts = {"lat": lax.axis_size("lat"), "lon": lax.axis_size("lon")}
-    kinds = [kind for kind, _ in pairs]
-    arrays = [array for _, array in pairs]
+def exchange(ident, per_dev, *jobs):
+    counts = {"lat": lax.axis_size("lat"), "lon": lax.axis_size("lon"), "orders": per_dev}
+    kinds = [kind for kind, _, _ in jobs]
+    reaches = [reach for _, reach, _ in jobs]
+    arrays = [array for _, _, array in jobs]
     dma = pltpu.SemaphoreType.DMA
     shapes, scratch, lengths = [], [], []
-    for kind, array in pairs:
+    for kind, reach, array in jobs:
         shape = array.shape
-        held = [dma, dma((2, counts["lat"]))]
-        if kind is not Swap:
+        chunks = 1 if reach is None else per_dev // PAIR
+        while chunks % 2 == 0 and counts["lon"] * counts["lat"] * chunks > 1024:
+            chunks //= 2
+        held = [dma, dma((2, counts["lat"], chunks))]
+        if kind is Spread:
+            held.append(dma((2, counts["lon"], counts["lat"], chunks)))
+        if kind is Reduce:
             held.append(dma((2, counts["lon"], counts["lat"])))
         if kind is Spread:
             shape = (counts["lon"],) + shape
@@ -303,7 +358,7 @@
         scratch += held
         lengths.append(len(held))
     return pl.pallas_call(
-        functools.partial(exchange_kernel, kinds, counts, lengths),
+        functools.partial(exchange_kernel, kinds, reaches, counts, lengths),
         out_shape=shapes,
         in_specs=[ANY] * len(arrays),
         out_specs=[ANY] * len(arrays),
@@ -351,76 +406,105 @@
     )(scale, table, field)
 
 
-def transform_kernel(forward, legendre_ref, scale_ref, in_ref, out_ref, in_rows, out_rows):
+def analyse_kernel(legendre_ref, in_ref, out_ref, in_rows, out_rows):
     orders, degrees, count_lat = legendre_ref.shape
-    taken, given = (count_lat, degrees) if forward else (degrees, count_lat)
     width = in_ref.shape[1]
     in_rows[...] = in_ref[...].astype(jnp.float32)
     for order in range(orders):
-        piece = [in_rows[pl.ds(2 * order + r, taken, stride=2 * orders), :] for r in range(2)]
+        piece = [in_rows[pl.ds(2 * order + r, count_lat, stride=2 * orders), :] for r in range(2)]
+        value = jnp.dot(
+            legendre_ref[order],
+            jnp.concatenate(piece, axis=1).astype(jnp.bfloat16),
+            preferred_element_type=jnp.float32,
+        )
+        for owner in range(degrees // orders):
+            for r in range(2):
+                place = ((owner * orders + order) * 2 + r) * orders
+                out_rows[place : place + orders, :] = value[
+                    owner * orders : (owner + 1) * orders, r * width : (r + 1) * width
+                ]
+    out_ref[...] = out_rows[...].astype(jnp.bfloat16)
+
+
+def analyse(legendre, rows):
+    orders, degrees, _ = legendre.shape
+    shape = (2 * orders * degrees, rows.shape[1])
+    return pl.pallas_call(
+        analyse_kernel,
+        out_shape=jax.ShapeDtypeStruct(shape, jnp.bfloat16),
+        in_specs=[VMEM] * 2,
+        out_specs=VMEM,
+        scratch_shapes=[pltpu.VMEM(rows.shape, jnp.float32), pltpu.VMEM(shape, jnp.float32)],
+        compiler_params=limits(),
+    )(legendre, rows)
+
+
+def synthesise_kernel(order_ref, legendre_ref, scale_ref, in_ref, out_ref, in_rows, held, out_rows):
+    orders, degrees, count_lat = legendre_ref.shape
+    width = in_ref.shape[1]
+    in_rows[...] = in_ref[...].astype(jnp.float32)
+    degree = lax.broadcasted_iota(jnp.int32, held.shape, 0)
+    for order in range(orders):
+        for owner in range(degrees // orders):
+            for r in range(2):
+                place = ((owner * orders + order) * 2 + r) * orders
+                held[owner * orders : (owner + 1) * orders, r * width : (r + 1) * width] = in_rows[
+                    place : place + orders, :
+                ]
+        piece = jnp.where(degree >= order_ref[order], held[...], 0.0).astype(jnp.bfloat16)
         value = lax.dot_general(
             legendre_ref[order],
-            jnp.concatenate(piece, axis=1).astype(jnp.bfloat16),
-            (((1 if forward else 0,), (0,)), ((), ())),
+            piece,
+            (((0,), (0,)), ((), ())),
             preferred_element_type=jnp.float32,
         )
-        if not forward:
-            value = value * scale_ref[...]
+        value = value * scale_ref[...]
         for r in range(2):
-            out_rows[pl.ds(2 * order + r, given, stride=2 * orders), :] = value[
+            out_rows[pl.ds(2 * order + r, count_lat, stride=2 * orders), :] = value[
                 :, r * width : (r + 1) * width
             ]
     out_ref[...] = out_rows[...].astype(jnp.bfloat16)
 
 
-def transform(forward, legendre, scale, rows):
+def synthesise(order_ids, legendre, scale, rows):
     orders, degrees, count_lat = legendre.shape
-    height = 2 * orders * (degrees if forward else count_lat)
-    return pl.pallas_call(
-        functools.partial(transform_kernel, forward),
-        out_shape=jax.ShapeDtypeStruct((height, rows.shape[1]), jnp.bfloat16),
-        in_specs=[VMEM] * 3,
+    shape = (2 * orders * count_lat, rows.shape[1])
+    return pl.pallas_call(
+        synthesise_kernel,
+        out_shape=jax.ShapeDtypeStruct(shape, jnp.bfloat16),
+        in_specs=[SMEM] + [VMEM] * 3,
         out_specs=VMEM,
         scratch_shapes=[
             pltpu.VMEM(rows.shape, jnp.float32),
-            pltpu.VMEM((height, rows.shape[1]), jnp.float32),
+            pltpu.VMEM((degrees, 2 * rows.shape[1]), jnp.float32),
+            pltpu.VMEM(shape, jnp.float32),
         ],
         compiler_params=limits(),
-    )(legendre, scale, rows)
-
-
-def degree_rows(ref, lead, pair, depth):
-    block = ref[lead + (slice(None), slice(pair * PAIR * depth, (pair + 1) * PAIR * depth))]
-    block = block.astype(jnp.float32)
-    count, _, width = block.shape
-    return [
-        block[:, i * depth : (i + 1) * depth].reshape(count * depth, width).astype(jnp.bfloat16)
-        for i in range(PAIR)
-    ]
-
-
-def all_channels(ref, pair, depth):
-    owners = [degree_rows(ref, (o,), pair, depth) for o in range(ref.shape[0])]
-    return [jnp.concatenate([rows[i] for rows in owners], axis=1) for i in range(PAIR)]
-
-
-def mix_kernel(adjoint_ref, mixing_ref, out_ref):
+    )(order_ids, legendre, scale, rows)
+
+
+def degree_rows(ref, degree, degrees, part):
+    depth = 2 * degrees
+    return pl.ds(part * degrees + degree, ref.shape[0] // depth, stride=depth)
+
+
+def mix_kernel(adjoint_ref, mixing_ref, out_ref, in_rows, out_rows):
     degrees, width = mixing_ref.shape[:2]
-    _, lat_count, height, _ = adjoint_ref.shape
-    depth = height // degrees
-    for pair in range(degrees // PAIR):
-        values = []
-        for i, full in enumerate(all_channels(adjoint_ref, pair, depth)):
+    for owner in range(adjoint_ref.shape[0]):
+        in_rows[...] = adjoint_ref[owner].astype(jnp.float32)
+        for degree in range(degrees):
+            places = [degree_rows(in_rows, degree, degrees, r) for r in range(2)]
+            own = jnp.concatenate([in_rows[place, :] for place in places], axis=0)
             value = lax.dot_general(
-                full,
-                mixing_ref[pair * PAIR + i],
+                own.astype(jnp.bfloat16),
+                mixing_ref[degree, :, owner * width : (owner + 1) * width],
                 (((1,), (1,)), ((), ())),
                 preferred_element_type=jnp.float32,
             )
-            values.append(value.reshape(lat_count, depth, width))
-        out_ref[:, pair * PAIR * depth : (pair + 1) * PAIR * depth, :] = jnp.concatenate(
-            values, axis=1
-        ).astype(jnp.bfloat16)
+            for r, place in enumerate(places):
+                half = value[r * place.size : (r + 1) * place.size]
+                out_rows[place, :] = half if owner == 0 else out_rows[place, :] + half
+    out_ref[...] = out_rows[...].astype(jnp.bfloat16)
 
 
 def mix(adjoint, mixing):
@@ -429,31 +513,44 @@
         out_shape=jax.ShapeDtypeStruct(adjoint.shape[1:], jnp.bfloat16),
         in_specs=[VMEM] * 2,
         out_specs=VMEM,
+        scratch_shapes=[pltpu.VMEM(adjoint.shape[1:], jnp.float32)] * 2,
         compiler_params=limits(),
     )(adjoint, mixing)
 
 
-def weight_kernel(adjoint_ref, coefficient_ref, out_ref):
-    degrees = out_ref.shape[0]
-    depth = adjoint_ref.shape[2] // degrees
-    for pair in range(degrees // PAIR):
-        full = all_channels(adjoint_ref, pair, depth)
-        own = degree_rows(coefficient_ref, (), pair, depth)
-        for i in range(PAIR):
-            out_ref[pair * PAIR + i] = lax.dot_general(
-                own[i], full[i], (((0,), (0,)), ((), ())), preferred_element_type=jnp.float32
+def weight_kernel(first_ref, order_ref, adjoint_ref, coefficient_ref, out_ref, other_rows, own_rows):
+    degrees, width = out_ref.shape[:2]
+    own_rows[...] = coefficient_ref[...].astype(jnp.float32)
+
+    def read(rows, degree):
+        kept = order_ref[...] <= first_ref[0] + degree
+        pieces = [
+            jnp.where(kept, rows[degree_rows(rows, degree, degrees, r), :], 0.0) for r in range(2)
+        ]
+        return jnp.concatenate(pieces, axis=0).astype(jnp.bfloat16)
+
+    for owner in range(adjoint_ref.shape[0]):
+        other_rows[...] = adjoint_ref[owner].astype(jnp.float32)
+        for degree in range(degrees):
+            out_ref[degree, :, owner * width : (owner + 1) * width] = lax.dot_general(
+                read(own_rows, degree),
+                read(other_rows, degree),
+                (((0,), (0,)), ((), ())),
+                preferred_element_type=jnp.float32,
             )
 
 
-def weight_gradient(adjoint, coefficients, degrees):
-    lon_count, _, _, width = adjoint.shape
+def weight_gradient(first, order_ids, adjoint, coefficients, degrees):
+    lon_count, _, width = adjoint.shape
+    order_rows = jnp.broadcast_to(order_ids[:, None], (order_ids.shape[0], width))
     return pl.pallas_call(
         weight_kernel,
         out_shape=jax.ShapeDtypeStruct((degrees, width, lon_count * width), jnp.float32),
-        in_specs=[VMEM] * 2,
+        in_specs=[SMEM] + [VMEM] * 3,
         out_specs=VMEM,
+        scratch_shapes=[pltpu.VMEM(coefficients.shape, jnp.float32)] * 2,
         compiler_params=limits(),
-    )(adjoint, coefficients)
+    )(first[None], order_rows, adjoint, coefficients)
 
 
 def grid_kernel(table_ref, back_ref, field_ref, out_ref):
@@ -503,30 +600,43 @@
     lat_pos = lax.axis_index("lat")
     lon_pos = lax.axis_index("lon")
     slot_ids = jnp.arange(order_total, dtype=jnp.int32)
-    forward, backward = fourier_tables(slot_ids, lon_pos * lon_rows, lon_rows, count_lon)
+    slot_ids = slot_ids // per_dev + lat_count * (slot_ids % per_dev)
+    forward, forward_rows, backward_rows = fourier_tables(
+        slot_ids, lon_pos * lon_rows, lon_rows, count_lon
+    )
     weights = quadrature(count_lat)
     own_weights = lax.dynamic_slice_in_dim(weights, lat_pos * lat_rows, lat_rows)
-    own_orders = lat_pos * per_dev + jnp.arange(per_dev, dtype=jnp.int32)
+    own_orders = lat_pos + lat_count * jnp.arange(per_dev, dtype=jnp.int32)
     legendre = legendre_table(own_orders, count_lat, order_total, order_total)
     scale = weights[:, None]
     by_lat = (lat_count, -1, block_ch)
+    by_both = (lon_count, -1, block_ch)
     flat = (-1, block_ch)
 
     part_g = partial_spectrum(
-        cotangent, backward.T, jnp.ones_like(own_weights), lat_count, lon_count
+        cotangent, backward_rows, jnp.ones_like(own_weights), lat_count, lon_count
     )
-    (rows_g,) = exchange(0, (Reduce, part_g))
-    part_x = partial_spectrum(grid_input, forward.T, own_weights, lat_count, lon_count)
-    adjoint = transform(True, legendre, scale, rows_g.reshape(flat))
-    adjoint, rows_x = exchange(1, (Spread, adjoint.reshape(by_lat)), (Reduce, part_x))
-    (mixed,) = exchange(2, (Swap, mix(adjoint, mixing)))
-    back = transform(False, legendre, scale, mixed.reshape(flat))
-    coefficients = transform(True, legendre, scale, rows_x.reshape(flat))
+    (rows_g,) = exchange(0, per_dev, (Reduce, None, part_g))
+    part_x = partial_spectrum(grid_input, forward_rows, own_weights, lat_count, lon_count)
+    adjoint = analyse(legendre, rows_g.reshape(flat))
+    adjoint, rows_x = exchange(
+        1, per_dev, (Spread, "out", adjoint.reshape(by_lat)), (Reduce, None, part_x)
+    )
+    adjoint = adjoint.reshape(by_both)
+    mixed = mix(adjoint, mixing)
+    (mixed,) = exchange(2, per_dev, (Swap, "home", mixed.reshape(by_lat)))
+    back = synthesise(own_orders, legendre, scale, mixed.reshape(flat))
+    coefficients = analyse(legendre, rows_x.reshape(flat))
     back, coefficients = exchange(
-        3, (Spread, back.reshape(by_lat)), (Swap, coefficients.reshape(by_lat))
+        3,
+        per_dev,
+        (Spread, None, back.reshape(by_lat)),
+        (Swap, "out", coefficients.reshape(by_lat)),
     )
     input_grad = grid_gradient(forward, back, cotangent)
-    weight_grad = weight_gradient(adjoint, coefficients, per_dev)
+    weight_grad = weight_gradient(
+        lat_pos * per_dev, slot_ids, adjoint, coefficients.reshape(flat), per_dev
+    )
     return (input_grad, weight_grad)
 
 

time: 322 us -> 327 us (1.016)
  other arithmetic: 3.77 us -> 11.4 us
  local copies, waits for them, and re-layouts: 11.1 us -> 4.43 us
  Pallas kernels: 305 us -> 310 us
    convert_element_type x0 -> x2, other arithmetic: none -> 10.3 us  [fourier_tables(): return tuple((table.astype(jnp.bfloat16) for table in tables))]
where the time goes in v4:
time: 327 us
  Pallas kernels  310 us (95%)
  other arithmetic  11.4 us (3%)
  local copies, waits for them, and re-layouts  4.43 us (1%)
    pallas_call x4, Pallas kernels, exchange(): pl.pallas_call(functools.partial(exchange_kernel, kinds, reaches, counts,...  262 us
    pallas_call x2, Pallas kernels, partial_spectrum(): pl.pallas_call(functools.partial(spectrum_kernel, lon_count), grid=(rows...  19.7 us
    pallas_call x1, Pallas kernels, grid_gradient(): pl.pallas_call(grid_kernel, grid=(rows // PAIR,), out_shape=jax.ShapeDtyp...  12.4 us
    convert_element_type x2, other arithmetic, fourier_tables(): return tuple((table.astype(jnp.bfloat16) for table in tables))  10.3 us

profile of v4, /device:TPU:27, one launch (start us, length us, event | category | flops | bytes accessed | tf_op | source)
XLA Modules:
  0.0 326.6 jit_solution(129413438195444620)
XLA Ops:
  0.7 0.1 multiply_cosine_fusion.cosine_ref
  0.8 0.1 dynamic_slice.3.scale_ref
  0.9 0.2 select_reduce_fusion
  1.2 0.1 multiply_add_fusion.start_ref
  1.2 0.1 broadcast_in_dim.53.order_ref
  1.3 0.1 broadcast_in_dim.47
  1.4 0.1 mul.186
  1.6 0.6 sine_multiply_fusion.scale_ref
  2.2 4.9 %fusion.9.table_ref = bf16[720,384]{1,0:T(8,128)(2,1)S(1)} fusion(s32[384]{0:T(512)S(1)} %fusion.14, s32[384]{0:T(512)S(1)} %mul.186, s32[720]{0:T(1024)S(1)} %iota_add_fusion), kind=kLoop, calls=%fused_computation.13 | loop fusion | flops 3317760 | bytes 558912 | tf_op jit(solution)/shard_map/convert_element_type | solution.py:94
  7.1 5.4 %fusion.13 = (bf16[384,720]{1,0:T(8,128)(2,1)S(1)}, bf16[384,720]{1,0:T(8,128)(2,1)S(1)}) fusion(s32[384]{0:T(512)S(1)} %fusion.14, s32[384]{0:T(512)S(1)} %mul.186, s32[720]{0:T(1024)S(1)} %iota_add_fusion, f32[384]{0:T(512)S(1)} %select_multiply_fusion), kind=kLoop, calls=%fused_computation.18 | loop fusion | flops 3870720 | bytes 1113408 | tf_op jit(solution)/shard_map/convert_element_type | solution.py:94
  12.6 5.3 %shard_map.50.legendre_ref = bf16[12,192,352]{2,1,0:T(8,128)(2,1)S(1)} custom-call(f32[12,1]{1,0:T(8,128)S(1)} %add_convert_fusion.order_ref, f32[1,352]{1,0:T(1,128)S(1)} %multiply_cosine_fusion.cosine_ref, f32[12,352]{1,0:T(8,128)S(1)} %multiply_add_fusion.start_ref), custom_call_target="tpu_custom_call" | custom-call | tf_op jit(solution)/shard_map/pallas_call | solution.py:72
  17.9 9.9 %shard_map.54.refs_1_ = bf16[2,16,528,128]{3,2,1,0:T(8,128)(2,1)S(1)} custom-call(f32[22]{0:T(128)S(1)} %dynamic_slice.3.scale_ref, bf16[384,720]{1,0:T(8,128)(2,1)S(1)} %get-tuple-element.10.table_ref, bf16[22,720,256]{2,1,0:T(8,128)(2,1)} %field_ref.4), custom_call_target="tpu_custom_call" | custom-call | tf_op jit(solution)/shard_map/pallas_call | solution.py:393
  27.7 0.0 copy-start.1
  27.7 2.0 copy-done.1
  29.7 9.9 %shard_map.51.refs_0_ = bf16[2,16,528,128]{3,2,1,0:T(8,128)(2,1)S(1)} custom-call(f32[22]{0:T(128)S(1)} %broadcast_14_scale_ref.2.scale_ref, bf16[384,720]{1,0:T(8,128)(2,1)S(1)} %get-tuple-element.11.table_ref, bf16[22,720,256]{2,1,0:T(8,128)(2,1)} %field_ref.5), custom_call_target="tpu_custom_call" | custom-call | tf_op jit(solution)/shard_map/pallas_call | solution.py:393
  39.6 0.0 copy-start
  39.6 2.0 copy-done
  41.6 64.7 %shard_map.52 = bf16[16,528,128]{2,1,0:T(8,128)(2,1)S(1)} custom-call(bf16[2,16,528,128]{3,2,1,0:T(8,128)(2,1)} %copy-done), custom_call_target="tpu_custom_call" | custom-call | tf_op jit(solution)/shard_map/pallas_call | solution.py:360
  106.3 1.4 shard_map.53
  107.7 81.7 %shard_map.55 = (bf16[2,16,288,128]{3,2,1,0:T(8,128)(2,1)S(1)}, bf16[16,528,128]{2,1,0:T(8,128)(2,1)S(1)}) custom-call(bf16[16,288,128]{2,1,0:T(8,128)(2,1)S(1)} %bitcast.15, bf16[2,16,528,128]{3,2,1,0:T(8,128)(2,1)} %copy-done.1), custom_call_target="tpu_custom_call" | custom-call | tf_op jit(solution)/shard_map/pallas_call | solution.py:360
  189.4 0.0 copy-start.3
  189.4 1.4 shard_map.59
  190.7 0.0 copy-done.3
  190.8 2.1 shard_map.56
  192.9 21.4 %shard_map.57 = bf16[16,288,128]{2,1,0:T(8,128)(2,1)S(1)} custom-call(bf16[16,288,128]{2,1,0:T(8,128)(2,1)S(1)} %bitcast.17), custom_call_target="tpu_custom_call" | custom-call | tf_op jit(solution)/shard_map/pallas_call | solution.py:360
  214.3 2.4 shard_map.58
  216.7 93.8 %shard_map.60 = (bf16[2,16,528,128]{3,2,1,0:T(8,128)(2,1)}, bf16[16,288,128]{2,1,0:T(8,128)(2,1)S(1)}) custom-call(bf16[16,528,128]{2,1,0:T(8,128)(2,1)S(1)} %bitcast.13, bf16[16,288,128]{2,1,0:T(8,128)(2,1)S(1)} %bitcast.14), custom_call_target="tpu_custom_call" | custom-call | tf_op jit(solution)/shard_map/pallas_call | solution.py:360
  310.5 0.0 copy-start.2
  310.5 3.7 %shard_map.62 = f32[12,128,256]{2,1,0:T(8,128)} custom-call(s32[1]{0:T(128)} %bitcast.8.first_ref, s32[192,128]{1,0:T(8,128)S(1)} %broadcast_in_dim.53.order_ref, bf16[2,4608,128]{2,1,0:T(8,128)(2,1)S(1)} %bitcast.11, bf16[4608,128]{1,0:T(8,128)(2,1)S(1)} %bitcast.19), custom_call_target="tpu_custom_call" | custom-call | tf_op jit(solution)/shard_map/pallas_call | solution.py:546
  314.2 0.0 copy-done.2
  314.2 12.4 %shard_map.61 = bf16[22,720,256]{2,1,0:T(8,128)(2,1)} custom-call(bf16[720,384]{1,0:T(8,128)(2,1)S(1)} %fusion.9.table_ref, bf16[2,16,528,128]{3,2,1,0:T(8,128)(2,1)S(1)} %copy-done.2, bf16[22,720,256]{2,1,0:T(8,128)(2,1)} %field_ref.5), custom_call_target="tpu_custom_call" | custom-call | tf_op jit(solution)/shard_map/pallas_call | solution.py:575
  (11 shorter events, 0.2 us)
Async XLA Ops:
  27.7 2.0 copy-start.1
  39.6 2.1 copy-start
  189.4 1.4 copy-start.3
  310.5 3.7 %copy-start.2 = (bf16[2,16,528,128]{3,2,1,0:T(8,128)(2,1)S(1)}, bf16[2,16,528,128]{3,2,1,0:T(8,128)(2,1)}, u32[]{:S(2)}) copy-start(bf16[2,16,528,128]{3,2,1,0:T(8,128)(2,1)} %get-tuple-element.8.back_ref) | copy-start | bytes 12976132

commit v5 on v3

--- a/solution.py
+++ b/solution.py
@@ -147,6 +147,14 @@
         self.each(lambda copy: copy.wait())
 
 
+class Later(Swap):
+    def start(self):
+        self.own.start()
+
+    def step(self, offset):
+        self.copy(offset).start()
+
+
 class Spread(Swap):
     def __init__(self, counts, source, target, own_sem, sems, further):
         super().__init__(
@@ -261,7 +269,7 @@
     jobs, place = [], 0
     for kind, length, source, target in zip(kinds, lengths, sources, targets):
         held = scratch[place : place + length]
-        landing = (target,) if kind is Swap else ()
+        landing = (target,) if kind in (Swap, Later) else ()
         jobs.append(kind(counts, source, target, *landing, *held))
         place += length
     for job in jobs:
@@ -290,7 +298,7 @@
     for kind, array in pairs:
         shape = array.shape
         held = [dma, dma((2, counts["lat"]))]
-        if kind is not Swap:
+        if kind in (Spread, Reduce):
             held.append(dma((2, counts["lon"], counts["lat"])))
         if kind is Spread:
             shape = (counts["lon"],) + shape
@@ -330,8 +338,10 @@
         out_ref[owner] = jnp.concatenate(piece, axis=1).astype(jnp.bfloat16)
 
 
-def partial_spectrum(field, table, scale, lat_count, lon_count):
-    rows, points, channels = field.shape
+def partial_spectrum(field, table, scale, lat_count, lon_count, begin=0, end=None):
+    _, points, channels = field.shape
+    end = field.shape[0] if end is None else end
+    rows = end - begin
     orders = table.shape[0] // lat_count
     width = channels // lon_count
     block = (lon_count, lat_count, PAIR * orders, width)
@@ -344,11 +354,11 @@
         in_specs=[
             SMEM,
             pl.BlockSpec(table.shape, lambda i: (0, 0)),
-            pl.BlockSpec((PAIR, points, channels), lambda i: (i, 0, 0)),
+            pl.BlockSpec((PAIR, points, channels), lambda i: (i + begin // PAIR, 0, 0)),
         ],
         out_specs=pl.BlockSpec(block, lambda i: (0, 0, i, 0)),
         compiler_params=limits(),
-    )(scale, table, field)
+    )(scale[begin:end], table, field)
 
 
 def transform_kernel(forward, legendre_ref, scale_ref, in_ref, out_ref, in_rows, out_rows):
@@ -516,14 +526,19 @@
         cotangent, backward.T, jnp.ones_like(own_weights), lat_count, lon_count
     )
     (rows_g,) = exchange(0, (Reduce, part_g))
-    part_x = partial_spectrum(grid_input, forward.T, own_weights, lat_count, lon_count)
+    middle = lat_rows // PAIR // 2 * PAIR
+    parts_x = [
+        partial_spectrum(grid_input, forward.T, own_weights, lat_count, lon_count, *rows)
+        for rows in ((0, middle), (middle, lat_rows))
+    ]
     adjoint = transform(True, legendre, scale, rows_g.reshape(flat))
-    adjoint, rows_x = exchange(1, (Spread, adjoint.reshape(by_lat)), (Reduce, part_x))
-    (mixed,) = exchange(2, (Swap, mix(adjoint, mixing)))
+    adjoint, upper_x = exchange(1, (Spread, adjoint.reshape(by_lat)), (Reduce, parts_x[0]))
+    mixed, lower_x = exchange(2, (Swap, mix(adjoint, mixing)), (Reduce, parts_x[1]))
+    rows_x = jnp.concatenate([upper_x, lower_x], axis=1)
     back = transform(False, legendre, scale, mixed.reshape(flat))
     coefficients = transform(True, legendre, scale, rows_x.reshape(flat))
     back, coefficients = exchange(
-        3, (Spread, back.reshape(by_lat)), (Swap, coefficients.reshape(by_lat))
+        3, (Spread, back.reshape(by_lat)), (Later, coefficients.reshape(by_lat))
     )
     input_grad = grid_gradient(forward, back, cotangent)
     weight_grad = weight_gradient(adjoint, coefficients, per_dev)

time: 322 us -> 322 us (level)
    pallas_call x2 -> x3, Pallas kernels: 19.7 us -> 20.3 us  [partial_spectrum(): pl.pallas_call(functools.partial(spectrum_kernel, lon_count), grid=(rows...]
where the time goes in v5:
time: 322 us; the launch traced here: 321 us
  Pallas kernels  307 us (95%)
  local copies, waits for them, and re-layouts  9.65 us (3%)
  other arithmetic  3.91 us (1%)
    pallas_call x4, Pallas kernels, exchange(): pl.pallas_call(functools.partial(exchange_kernel, kinds, counts, lengths)...  261 us
    pallas_call x3, Pallas kernels, partial_spectrum(): pl.pallas_call(functools.partial(spectrum_kernel, lon_count), grid=(rows...  20.3 us
    pallas_call x1, Pallas kernels, grid_gradient(): pl.pallas_call(grid_kernel, grid=(rows // PAIR,), out_shape=jax.ShapeDtyp...  12.4 us

profile of v5, /device:TPU:27, one launch (start us, length us, event | category | flops | bytes accessed | tf_op | source)
XLA Modules:
  0.0 321.1 jit_solution(11915603612769369523)
XLA Ops:
  0.8 0.1 dynamic_slice.3
  0.9 0.1 slice.7.scale_ref
  1.0 0.2 select_reduce_fusion
  1.2 0.1 multiply_add_fusion.start_ref
  1.3 0.1 broadcast_in_dim.32
  1.4 0.1 mul.143
  1.5 0.6 sine_multiply_fusion.scale_ref
  2.2 2.5 fusion.5
  4.7 0.1 pad_maximum_fusion.1
  4.7 1.9 copy.14
  6.7 2.1 reshape.178
  8.8 0.3 copy.15.table_ref
  9.1 0.1 fusion.2.table_ref
  9.2 0.3 copy.16.table_ref
  9.4 5.3 %shard_map.50.legendre_ref = bf16[12,192,352]{2,1,0:T(8,128)(2,1)S(1)} custom-call(f32[12,1]{1,0:T(8,128)S(1)} %add_convert_fusion.order_ref, f32[1,352]{1,0:T(1,128)S(1)} %multiply_cosine_fusion.cosine_ref, f32[12,352]{1,0:T(8,128)S(1)} %multiply_add_fusion.start_ref), custom_call_target="tpu_custom_call" | custom-call | tf_op jit(solution)/shard_map/pallas_call | solution.py:72
  14.7 4.9 %shard_map.54.refs_1_ = bf16[2,16,240,128]{3,2,1,0:T(8,128)(2,1)S(1)} custom-call(f32[10]{0:T(128)S(1)} %bitcast.19, bf16[384,720]{1,0:T(8,128)(2,1)S(1)} %copy.16.table_ref, bf16[22,720,256]{2,1,0:T(8,128)(2,1)} %field_ref.6), custom_call_target="tpu_custom_call" | custom-call | tf_op jit(solution)/shard_map/pallas_call | solution.py:348
  19.7 5.5 %shard_map.57.refs_1_ = bf16[2,16,288,128]{3,2,1,0:T(8,128)(2,1)S(1)} custom-call(f32[12]{0:T(128)S(1)} %slice.7.scale_ref, bf16[384,720]{1,0:T(8,128)(2,1)S(1)} %copy.16.table_ref, bf16[22,720,256]{2,1,0:T(8,128)(2,1)} %field_ref.6), custom_call_target="tpu_custom_call" | custom-call | tf_op jit(solution)/shard_map/pallas_call | solution.py:348
  25.2 9.9 %shard_map.51.refs_0_ = bf16[2,16,528,128]{3,2,1,0:T(8,128)(2,1)S(1)} custom-call(f32[22]{0:T(128)S(1)} %broadcast_7_scale_ref.2.scale_ref, bf16[384,720]{1,0:T(8,128)(2,1)S(1)} %fusion.2.table_ref, bf16[22,720,256]{2,1,0:T(8,128)(2,1)} %field_ref.7), custom_call_target="tpu_custom_call" | custom-call | tf_op jit(solution)/shard_map/pallas_call | solution.py:348
  35.1 2.0 copy-done
  37.1 64.6 %shard_map.52 = bf16[16,528,128]{2,1,0:T(8,128)(2,1)S(1)} custom-call(bf16[2,16,528,128]{3,2,1,0:T(8,128)(2,1)} %copy-done), custom_call_target="tpu_custom_call" | custom-call | tf_op jit(solution)/shard_map/pallas_call | solution.py:313
  101.7 1.5 shard_map.53
  103.3 52.6 %shard_map.55 = (bf16[2,16,288,128]{3,2,1,0:T(8,128)(2,1)}, bf16[16,240,128]{2,1,0:T(8,128)(2,1)S(1)}) custom-call(bf16[16,288,128]{2,1,0:T(8,128)(2,1)S(1)} %bitcast.17, bf16[2,16,240,128]{3,2,1,0:T(8,128)(2,1)S(1)} %shard_map.54.refs_1_), custom_call_target="tpu_custom_call" | custom-call | tf_op jit(solution)/shard_map/pallas_call | solution.py:313
  155.9 1.7 copy-done.1
  157.6 0.8 shard_map.56.refs_0_
  158.3 56.3 %shard_map.58 = (bf16[16,288,128]{2,1,0:T(8,128)(2,1)S(1)}, bf16[16,288,128]{2,1,0:T(8,128)(2,1)S(1)}) custom-call(bf16[16,288,128]{2,1,0:T(8,128)(2,1)S(1)} %shard_map.56.refs_0_, bf16[2,16,288,128]{3,2,1,0:T(8,128)(2,1)S(1)} %shard_map.57.refs_1_), custom_call_target="tpu_custom_call" | custom-call | tf_op jit(solution)/shard_map/pallas_call | solution.py:313
  214.6 1.8 shard_map.59
  216.4 0.1 pad_maximum_fusion
  216.6 1.5 shard_map.60
  218.1 87.8 %shard_map.61 = (bf16[2,16,528,128]{3,2,1,0:T(8,128)(2,1)}, bf16[16,288,128]{2,1,0:T(8,128)(2,1)S(1)}) custom-call(bf16[16,528,128]{2,1,0:T(8,128)(2,1)S(1)} %bitcast.12, bf16[16,288,128]{2,1,0:T(8,128)(2,1)S(1)} %bitcast.16), custom_call_target="tpu_custom_call" | custom-call | tf_op jit(solution)/shard_map/pallas_call | solution.py:313
  306.0 1.8 shard_map.63
  307.7 1.0 copy-done.3
  308.7 12.4 %shard_map.62 = bf16[22,720,256]{2,1,0:T(8,128)(2,1)} custom-call(bf16[720,384]{1,0:T(8,128)(2,1)S(1)} %copy.15.table_ref, bf16[2,16,528,128]{3,2,1,0:T(8,128)(2,1)S(1)} %copy-done.3, bf16[22,720,256]{2,1,0:T(8,128)(2,1)} %field_ref.7), custom_call_target="tpu_custom_call" | custom-call | tf_op jit(solution)/shard_map/pallas_call | solution.py:488
  (17 shorter events, 0.2 us)
Async XLA Ops:
  35.1 2.1 copy-start
  103.3 52.6 %copy-start.4 = (bf16[12,128,256]{2,1,0:T(8,128)(2,1)S(1)}, bf16[12,128,256]{2,1,0:T(8,128)(2,1)}, u32[]{:S(2)}) copy-start(bf16[12,128,256]{2,1,0:T(8,128)(2,1)} %mixing_ref.1) | copy-start | bytes 2359300
  155.9 1.7 copy-start.1
  218.1 87.8 %copy-start.2 = (bf16[2,16,288,128]{3,2,1,0:T(8,128)(2,1)S(1)}, bf16[2,16,288,128]{3,2,1,0:T(8,128)(2,1)}, u32[]{:S(2)}) copy-start(bf16[2,16,288,128]{3,2,1,0:T(8,128)(2,1)} %get-tuple-element.8.adjoint_ref) | copy-start | bytes 7077892
  305.9 2.8 copy-start.3

commit v6 on v3

--- a/solution.py
+++ b/solution.py
@@ -92,6 +92,7 @@
 
 
 MESH = pl.DeviceIdType.MESH
+WINDOW = 6
 VMEM = pl.BlockSpec(memory_space=pltpu.VMEM)
 SMEM = pl.BlockSpec(memory_space=pltpu.SMEM)
 ANY = pl.BlockSpec(memory_space=pl.ANY)
@@ -170,10 +171,19 @@
         for ahead in range(1, self.counts["lon"]):
             self.onward(0, ahead).start()
 
+    def start(self):
+        self.own.start()
+        for offset in range(1, min(WINDOW + 1, self.counts["lat"])):
+            self.copy(offset).start()
+
     def step(self, offset):
         self.copy(offset).wait_recv()
         for ahead in range(1, self.counts["lon"]):
             self.onward(offset, ahead).start()
+
+        @pl.when(offset + WINDOW < self.counts["lat"])
+        def _():
+            self.copy(offset + WINDOW).start()
 
     def finish(self):
         self.each(lambda copy: copy.wait_send())

time: 322 us -> 335 us (1.040)
  Pallas kernels: 305 us -> 318 us
    pallas_call x4, Pallas kernels: 260 us -> 273 us  [exchange(): pl.pallas_call(functools.partial(exchange_kernel, kinds, counts, lengths)...]
where the time goes in v6:
time: 335 us; the launch traced here: 334 us
  Pallas kernels  318 us (95%)
  local copies, waits for them, and re-layouts  11.1 us (3%)
  other arithmetic  3.77 us (1%)
    pallas_call x4, Pallas kernels, exchange(): pl.pallas_call(functools.partial(exchange_kernel, kinds, counts, lengths)...  273 us
    pallas_call x2, Pallas kernels, partial_spectrum(): pl.pallas_call(functools.partial(spectrum_kernel, lon_count), grid=(rows...  19.7 us
    pallas_call x1, Pallas kernels, grid_gradient(): pl.pallas_call(grid_kernel, grid=(rows // PAIR,), out_shape=jax.ShapeDtyp...  12.4 us

profile of v6, /device:TPU:27, one launch (start us, length us, event | category | flops | bytes accessed | tf_op | source)
XLA Modules:
  0.0 333.5 jit_solution(12004947395491693413)
XLA Ops:
  0.7 0.1 multiply_cosine_fusion.cosine_ref
  0.8 0.1 dynamic_slice.3.scale_ref
  0.9 0.2 select_reduce_fusion
  1.2 0.1 multiply_add_fusion.start_ref
  1.2 0.1 broadcast_in_dim.32
  1.3 0.1 mul.143
  1.5 0.6 sine_multiply_fusion.scale_ref
  2.1 2.5 fusion.5
  4.6 0.1 pad_maximum_fusion
  4.7 1.9 copy.11
  6.6 2.1 reshape.178
  8.7 0.3 copy.12.table_ref
  9.0 0.1 fusion.2.table_ref
  9.1 0.3 copy.13.table_ref
  9.4 5.3 %shard_map.50.legendre_ref = bf16[12,192,352]{2,1,0:T(8,128)(2,1)S(1)} custom-call(f32[12,1]{1,0:T(8,128)S(1)} %add_convert_fusion.order_ref, f32[1,352]{1,0:T(1,128)S(1)} %multiply_cosine_fusion.cosine_ref, f32[12,352]{1,0:T(8,128)S(1)} %multiply_add_fusion.start_ref), custom_call_target="tpu_custom_call" | custom-call | tf_op jit(solution)/shard_map/pallas_call | solution.py:72
  14.7 9.9 %shard_map.54.refs_1_ = bf16[2,16,528,128]{3,2,1,0:T(8,128)(2,1)S(1)} custom-call(f32[22]{0:T(128)S(1)} %dynamic_slice.3.scale_ref, bf16[384,720]{1,0:T(8,128)(2,1)S(1)} %copy.13.table_ref, bf16[22,720,256]{2,1,0:T(8,128)(2,1)} %field_ref.4), custom_call_target="tpu_custom_call" | custom-call | tf_op jit(solution)/shard_map/pallas_call | solution.py:348
  24.5 2.0 copy-done.1
  26.5 9.9 %shard_map.51.refs_0_ = bf16[2,16,528,128]{3,2,1,0:T(8,128)(2,1)S(1)} custom-call(f32[22]{0:T(128)S(1)} %broadcast_7_scale_ref.2.scale_ref, bf16[384,720]{1,0:T(8,128)(2,1)S(1)} %fusion.2.table_ref, bf16[22,720,256]{2,1,0:T(8,128)(2,1)} %field_ref.5), custom_call_target="tpu_custom_call" | custom-call | tf_op jit(solution)/shard_map/pallas_call | solution.py:348
  36.4 0.0 copy-start
  36.4 2.0 copy-done
  38.4 64.6 %shard_map.52 = bf16[16,528,128]{2,1,0:T(8,128)(2,1)S(1)} custom-call(bf16[2,16,528,128]{3,2,1,0:T(8,128)(2,1)} %copy-done), custom_call_target="tpu_custom_call" | custom-call | tf_op jit(solution)/shard_map/pallas_call | solution.py:315
  103.0 1.5 shard_map.53
  104.6 78.8 %shard_map.55 = (bf16[2,16,288,128]{3,2,1,0:T(8,128)(2,1)S(1)}, bf16[16,528,128]{2,1,0:T(8,128)(2,1)S(1)}) custom-call(bf16[16,288,128]{2,1,0:T(8,128)(2,1)S(1)} %bitcast.16, bf16[2,16,528,128]{3,2,1,0:T(8,128)(2,1)} %copy-done.1), custom_call_target="tpu_custom_call" | custom-call | tf_op jit(solution)/shard_map/pallas_call | solution.py:315
  183.4 0.0 copy-start.3
  183.5 1.5 shard_map.59
  185.0 0.8 shard_map.56.refs_0_
  185.8 30.0 %shard_map.57 = bf16[16,288,128]{2,1,0:T(8,128)(2,1)S(1)} custom-call(bf16[16,288,128]{2,1,0:T(8,128)(2,1)S(1)} %shard_map.56.refs_0_), custom_call_target="tpu_custom_call" | custom-call | tf_op jit(solution)/shard_map/pallas_call | solution.py:315
  215.8 1.8 shard_map.58
  217.6 99.6 %shard_map.60 = (bf16[2,16,528,128]{3,2,1,0:T(8,128)(2,1)}, bf16[16,288,128]{2,1,0:T(8,128)(2,1)S(1)}) custom-call(bf16[16,528,128]{2,1,0:T(8,128)(2,1)S(1)} %bitcast.11, bf16[16,288,128]{2,1,0:T(8,128)(2,1)S(1)} %bitcast.14), custom_call_target="tpu_custom_call" | custom-call | tf_op jit(solution)/shard_map/pallas_call | solution.py:315
  317.1 1.8 shard_map.62
  318.9 2.2 copy-done.2
  321.1 12.4 %shard_map.61 = bf16[22,720,256]{2,1,0:T(8,128)(2,1)} custom-call(bf16[720,384]{1,0:T(8,128)(2,1)S(1)} %copy.12.table_ref, bf16[2,16,528,128]{3,2,1,0:T(8,128)(2,1)S(1)} %copy-done.2, bf16[22,720,256]{2,1,0:T(8,128)(2,1)} %field_ref.5), custom_call_target="tpu_custom_call" | custom-call | tf_op jit(solution)/shard_map/pallas_call | solution.py:488
  (12 shorter events, 0.1 us)
Async XLA Ops:
  24.5 2.0 copy-start.1
  36.4 2.1 copy-start
  183.4 1.6 copy-start.3
  318.9 2.2 copy-start.2
